TPU v7x, 32 devices: a whole 2x2x4 slice. The times are simulated.
32 devices in a mesh: section: 2 (over y), dp: 4 (over x, core), mp: 4 (over z).
Axes of the slice: x: 2, y: 2, z: 4, core: 2. Of those that a mesh axis runs over, the one named last changes fastest.
Arguments:
- activations: bfloat16 [768, 27648], P(('dp', 'section'), 'mp'), may hold values from -6 to 6
- weight: bfloat16 [27648, 5120], P('mp', 'section'), may hold values from -0.0390625 to 0.0390625
- readout: bfloat16 [768, 5120], P('dp', 'section'), may hold values from -0.02734375 to 0.02734375
- logp_rest: float32 [768], P('dp'), may hold values from -1.2 to 1.2
- old_logp: float32 [768], P('dp'), may hold values from -1.2 to 1.2
- ref_logp: float32 [768], P('dp'), may hold values from -4 to 4
- lengths: int32 [2], replicated, may hold values from 1 to 384, as said below
- group_ids: int32 [2], replicated, may hold values from 0 to 0, as said below
- rewards: float32 [2], replicated, may hold values from -6 to 6
- first_moment: float32 [4, 6912, 5120], P('mp', 'dp', 'section'), may hold values from -0.0006 to 0.0006
- second_moment: float32 [4, 6912, 5120], P('mp', 'dp', 'section'), may hold values from 1e-10 to 1e-05
Outputs:
- new_weight: bfloat16 [27648, 5120], P('mp', 'section')
- new_first: float32 [4, 6912, 5120], P('mp', 'dp', 'section')
- new_second: float32 [4, 6912, 5120], P('mp', 'dp', 'section')
Inputs may be any that keep to these rules, and one draw needn't show every extreme that they name: `lengths`: every response has at least one live token, and some response has all 384 slots live. `group_ids`: each group id names exactly 2 responses.
All inputs are finite; a program needn't handle non-finite values.
Results may differ from a plain program's by a relative error of at most 0.015.
Values may be sent and summed in bfloat16 or wider, within the bound.
A program may use at most 256 MiB of HBM per device.

v0:
```python
import jax
import jax.numpy as jnp
from jax import lax
from jax.sharding import PartitionSpec as P

RESP_LEN = 384


clip_eps = 0.2
kl_coef = 0.1
beta_one = 0.9
beta_two = 0.95
adam_eps = 1e-08
learn_rate = 0.0003
weight_decay = 0.1
first_correct = 1.0 - 0.9**10
second_correct = 1.0 - 0.95**10


def token_terms(lengths, group_ids, rewards, positions, resp_len):
    total_resp = rewards.shape[0]
    members = (group_ids[:, None] == group_ids[None, :]).astype(jnp.float32)
    group_size = jnp.sum(members, axis=1)
    group_mean = jnp.sum(members * rewards[None, :], axis=1) / group_size
    deviation = rewards[None, :] - group_mean[:, None]
    group_spread = jnp.sqrt(jnp.sum(members * deviation * deviation, axis=1) / group_size)
    advantage = (rewards - group_mean) / jnp.maximum(group_spread, 1.0)
    response = positions // resp_len
    slot_index = (positions % resp_len).astype(jnp.float32)
    picker = (response[:, None] == jnp.arange(total_resp, dtype=jnp.int32)[None, :]).astype(
        jnp.float32
    )
    adv_token = jnp.sum(picker * advantage[None, :], axis=1)
    len_token = jnp.sum(picker * lengths.astype(jnp.float32)[None, :], axis=1)
    token_weight = jnp.where(slot_index < len_token, 1.0 / (len_token * total_resp), 0.0)
    return (adv_token, token_weight)


def token_loss(new_logp, old_logp, ref_logp, adv_token, token_weight):
    ratio = jnp.exp(new_logp - old_logp)
    surrogate = jnp.minimum(
        ratio * adv_token, jnp.clip(ratio, 1.0 - clip_eps, 1.0 + clip_eps) * adv_token
    )
    gap = ref_logp - new_logp
    kl_term = jnp.exp(gap) - gap - 1.0
    return jnp.sum(token_weight * (kl_coef * kl_term - surrogate))


def token_coeff(new_logp, old_logp, ref_logp, adv_token, token_weight):

    def loss_of(values):
        return token_loss(values, old_logp, ref_logp, adv_token, token_weight)

    _, pullback = jax.vjp(loss_of, new_logp)
    return pullback(jnp.float32(1.0))[0]


def adam_rows(weight_rows, first_rows, second_rows, gradient):
    new_first = beta_one * first_rows + (1.0 - beta_one) * gradient
    new_second = beta_two * second_rows + (1.0 - beta_two) * gradient * gradient
    current = weight_rows.astype(jnp.float32)
    update = (
        new_first / first_correct / (jnp.sqrt(new_second / second_correct) + adam_eps)
        + weight_decay * current
    )
    return ((current - learn_rate * update).astype(jnp.bfloat16), new_first, new_second)


def on_device(
    activations,
    weight,
    readout,
    logp_rest,
    old_logp,
    ref_logp,
    lengths,
    group_ids,
    rewards,
    first_moment,
    second_moment,
):
    gathered = lax.all_gather(activations, "section", axis=0, tiled=True)
    tok_rep = gathered.shape[0]
    layer_out = jnp.dot(gathered, weight, preferred_element_type=jnp.float32)
    score_share = jnp.sum(layer_out * readout.astype(jnp.float32), axis=1)
    score = lax.psum(score_share, ("section", "mp"))
    new_logp = logp_rest + score
    positions = lax.axis_index("dp") * tok_rep + jnp.arange(tok_rep, dtype=jnp.int32)
    adv_token, token_weight = token_terms(lengths, group_ids, rewards, positions, RESP_LEN)
    coeff = token_coeff(new_logp, old_logp, ref_logp, adv_token, token_weight)
    weighted = (coeff[:, None] * readout.astype(jnp.float32)).astype(jnp.bfloat16)
    shard_rows = first_moment.shape[1]
    owned = lax.all_to_all(gathered, "dp", split_axis=1, concat_axis=0, tiled=True)
    piece = lax.all_gather(weighted, "dp", axis=0, tiled=True)
    count = piece.shape[0]
    replicas = count // tok_rep
    left = owned.reshape(replicas, tok_rep, owned.shape[1])
    right = piece.reshape(replicas, tok_rep, piece.shape[1])
    parts = jnp.einsum("rts,rtd->rsd", left, right, preferred_element_type=jnp.float32)
    gradient = jnp.sum(parts.astype(jnp.bfloat16).astype(jnp.float32), axis=0)
    weight_rows = lax.dynamic_slice_in_dim(weight, lax.axis_index("dp") * shard_rows, shard_rows, 0)
    updated_rows, new_first, new_second = adam_rows(
        weight_rows, first_moment[0], second_moment[0], gradient
    )
    new_weight = lax.all_gather(updated_rows, "dp", axis=0, tiled=True)
    return (new_weight, new_first[None], new_second[None])


def solution(mesh):
    placed = (
        P(("dp", "section"), "mp"),
        P("mp", "section"),
        P("dp", "section"),
        P("dp"),
        P("dp"),
        P("dp"),
        P(),
        P(),
        P(),
        P("mp", "dp", "section"),
        P("mp", "dp", "section"),
    )
    return jax.shard_map(
        on_device,
        mesh=mesh,
        in_specs=placed,
        out_specs=(P("mp", "section"), P("mp", "dp", "section"), P("mp", "dp", "section")),
        check_vma=False,
    )
```

profile of v0, /device:TPU:1, one launch (start us, length us, event | category | flops | bytes accessed | tf_op | source)
XLA Modules:
  0.0 443.8 jit_solution(11469964612653099779)
XLA Ops:
  7.2 0.0 all-gather.4.cloned.1.call-start
  7.2 0.7 all-gather.4.cloned.1.call-update
  7.9 0.0 all-gather.6.cloned.1.call-start
  7.9 0.7 convert_element_type.33
  8.6 0.9 fusion.27
  9.6 0.9 fusion.16
  10.5 0.7 maximum_divide_fusion
  11.2 0.1 select_reduce_fusion.1
  11.3 0.0 copy-start.1
  11.3 0.0 copy-start.2
  11.3 0.0 copy-start.3
  11.3 0.0 copy-start
  11.3 39.7 %all-gather.4.cloned.1.call-done = bf16[192,6912]{1,0:T(8,128)(2,1)} async-done(((bf16[96,6912]{1,0:T(8,128)(2,1)}), bf16[192,6912]{1,0:T(8,128)(2,1)}) %all-gather.4.cloned.1.call-update) | async-done | bytes 2654224 | tf_op jit(solution)/shard_map/all_gather | solution.py:82
  51.1 15.7 %fusion.14 = f32[192]{0:T(256)S(1)} fusion(bf16[192,2560]{1,0:T(8,128)(2,1)} %param.13, bf16[192,6912]{1,0:T(8,128)(2,1)} %all-gather.4.cloned.1.call-done, bf16[6912,2560]{1,0:T(8,128)(2,1)} %param.12), kind=kOutput, calls=%fused_computation.24 | convolution fusion | flops 6796247040 | bytes 39027456 | tf_op jit(solution)/shard_map/dot_general | solution.py:84
  66.7 16.8 %psum.7 = f32[192]{0:T(256)S(1)} all-reduce(f32[192]{0:T(256)S(1)} %fusion.14), channel_id=1, replica_groups=mesh['section'=2,'dp'=4,'mp'=4] {'section','mp'}, use_global_device_ids=true, to_apply=%region_2.0 | all-reduce | flops 192 | bytes 1536 | tf_op jit(solution)/shard_map/psum | solution.py:86
  83.5 0.0 copy-done.1
  83.5 0.0 copy-done.2
  83.5 0.0 copy-done.3
  83.5 0.0 copy-done
  83.6 1.2 fusion.13
  84.7 0.0 all-gather.6.cloned.1.call-update
  84.8 6.1 %all_to_all.12 = bf16[192,4,1728]{2,1,0:T(4,128)(2,1)S(1)} reshape(bf16[192,6912]{1,0:T(8,128)(2,1)} %all-gather.4.cloned.1.call-done) | data formatting | bytes 5308416 | tf_op jit(solution)/shard_map/all_to_all | solution.py:93
  90.8 1.8 copy.15
  92.6 8.1 %all-to-all-start = ((bf16[192,4,1728]{2,0,1:T(8,128)(2,1)}), bf16[192,4,1728]{2,0,1:T(8,128)(2,1)S(1)}, u32[]{:S(2)}, u32[]{:S(2)}) async-start(bf16[192,4,1728]{2,0,1:T(8,128)(2,1)} %copy.15), calls=%async_computation | async-start | bytes 5505024 | tf_op jit(solution)/shard_map/all_to_all | solution.py:93
  100.7 0.0 all-gather.8.cloned.1.call-start
  100.7 47.1 %all-to-all-done = bf16[192,4,1728]{2,0,1:T(8,128)(2,1)S(1)} async-done(((bf16[192,4,1728]{2,0,1:T(8,128)(2,1)}), bf16[192,4,1728]{2,0,1:T(8,128)(2,1)S(1)}, u32[]{:S(2)}, u32[]{:S(2)}) %all-to-all-start) | async-done | bytes 2654240 | tf_op jit(solution)/shard_map/all_to_all | solution.py:93
  147.8 23.5 %convert_reduce_fusion = f32[2560,1728]{0,1:T(8,128)} fusion(bf16[4,192,2560]{2,1,0:T(8,128)(2,1)} %bitcast.26, bf16[192,4,1728]{2,0,1:T(8,128)(2,1)S(1)} %all-to-all-done), kind=kOutput, calls=%fused_computation | convolution fusion | flops 6843432960 | bytes 24281088 | tf_op jit(solution)/shard_map/rts,rtd->rsd/dot_general | solution.py:99
  171.3 27.2 %fusion.2 = bf16[1728,2560]{1,0:T(8,128)(2,1)} fusion(f32[2560,1728]{0,1:T(8,128)} %convert_reduce_fusion, f32[1,1728,2560]{2,1,0:T(8,128)} %param.21, f32[1,1728,2560]{2,1,0:T(8,128)} %param.20, bf16[6912,2560]{1,0:T(8,128)(2,1)} %param.12, s32[]{:T(128)S(6)} %select_n.51), kind=kLoop, calls=%fused_computation.8 | loop fusion | flops 75202560 | bytes 70778880 | tf_op jit(solution)/shard_map/convert_element_type | solution.py:66
  198.5 0.0 all-gather.8.cloned.1.call-update
  198.5 36.4 %fusion.8 = (f32[1,1728,2560]{2,1,0:T(8,128)}, f32[1,1728,2560]{2,1,0:T(8,128)}) fusion(f32[2560,1728]{0,1:T(8,128)} %convert_reduce_fusion, f32[1,1728,2560]{2,1,0:T(8,128)} %param.21, f32[1,1728,2560]{2,1,0:T(8,128)} %param.20), kind=kLoop, calls=%fused_computation.14 | loop fusion | flops 30965760 | bytes 88473600 | tf_op jit(solution)/shard_map/add | solution.py:60
  235.0 178.3 %all-gather.8.cloned.1.call-done = bf16[6912,2560]{1,0:T(8,128)(2,1)} async-done(((bf16[1728,2560]{1,0:T(8,128)(2,1)}), bf16[6912,2560]{1,0:T(8,128)(2,1)}) %all-gather.8.cloned.1.call-update) | async-done | bytes 35389456 | tf_op jit(solution)/shard_map/all_gather | solution.py:105
  413.3 24.0 %copy.17 = bf16[6912,2560]{1,0:T(8,128)(2,1)} copy(bf16[6912,2560]{1,0:T(8,128)(2,1)} %all-gather.8.cloned.1.call-done) | data formatting | bytes 70778880
  (4 shorter events, 0.1 us)
Async XLA Ops:
  7.2 43.9 %all-gather.4.cloned.1.call-start = ((), (), s32[]{:S(2)}) async-start(), calls=%async_computation.1 | async-start | bytes 3981312 | tf_op jit(solution)/shard_map/all_gather | solution.py:82
  7.9 139.9 %all-gather.6.cloned.1.call-start = ((), (), s32[]{:S(2)}) async-start(), calls=%async_computation.2 | async-start | bytes 4915200 | tf_op jit(solution)/shard_map/all_gather | solution.py:94
  11.3 72.2 %copy-start.1 = (f32[192]{0:T(256)S(1)}, f32[192]{0:T(256)}, u32[]{:S(2)}) copy-start(f32[192]{0:T(256)} %param.16) | copy-start | bytes 2308
  11.3 72.2 %copy-start.2 = (f32[192]{0:T(256)S(1)}, f32[192]{0:T(256)}, u32[]{:S(2)}) copy-start(f32[192]{0:T(256)} %param.15) | copy-start | bytes 2308
  11.3 72.2 %copy-start.3 = (f32[192]{0:T(256)S(1)}, f32[192]{0:T(256)}, u32[]{:S(2)}) copy-start(f32[192]{0:T(256)} %param.14) | copy-start | bytes 2308
  11.3 72.2 %copy-start = (bf16[192,2560]{1,0:T(8,128)(2,1)S(1)}, bf16[192,2560]{1,0:T(8,128)(2,1)}, u32[]{:S(2)}) copy-start(bf16[192,2560]{1,0:T(8,128)(2,1)} %param.13) | copy-start | bytes 2949124
  92.6 55.2 %all-to-all-start = ((bf16[192,4,1728]{2,0,1:T(8,128)(2,1)}), bf16[192,4,1728]{2,0,1:T(8,128)(2,1)S(1)}, u32[]{:S(2)}, u32[]{:S(2)}) async-start(bf16[192,4,1728]{2,0,1:T(8,128)(2,1)} %copy.15), calls=%async_computation | async-start | bytes 5505024 | tf_op jit(solution)/shard_map/all_to_all | solution.py:93
  100.7 312.5 %all-gather.8.cloned.1.call-start = ((), (), s32[]{:S(2)}) async-start(), calls=%async_computation.3 | async-start | bytes 44236800 | tf_op jit(solution)/shard_map/all_gather | solution.py:105
Sparse Core Ops, SparseCore 0:
  9.5 41.4 all-gather.3
  84.9 50.2 all-gather.5
  198.7 214.5 all-gather.7
where the time goes:
time: 444 us
  waiting for transfers between devices  266 us (60%)
  other arithmetic  68.1 us (15%)
  matrix products  39.2 us (9%)
  local copies, waits for them, and re-layouts  31.9 us (7%)
  blocking collectives  16.8 us (4%)
  between operations  13.8 us (3%)
  starting transfers between devices  8.19 us (2%)
    all_gather x1, waiting for transfers between devices, on_device(): new_weight = lax.all_gather(updated_rows, 'dp', axis=0, tiled=True)  178 us
    all_to_all x1, waiting for transfers between devices, on_device(): lax.all_to_all(gathered, 'dp', split_axis=1, concat_axis=0, tiled=True)  47.1 us
    all_gather x1, waiting for transfers between devices, on_device(): gathered = lax.all_gather(activations, 'section', axis=0, tiled=True)  39.7 us
    add x1, other arithmetic, adam_rows(): new_second = beta_two * second_rows + (1.0 - beta_two) * gradient * gradient  36.4 us
    convert_element_type x1, other arithmetic, adam_rows(): (current - learn_rate * update).astype(jnp.bfloat16)  27.2 us
    unnamed x9, local copies, waits for them, and re-layouts  24 us
    dot_general x1, matrix products, on_device(): jnp.einsum('rts,rtd->rsd', left, right, preferred_element_type=jnp.float32)  23.5 us
    psum x1, blocking collectives, on_device(): score = lax.psum(score_share, ('section', 'mp'))  16.8 us
  transfers between devices with their start and end apart: 4, of which 3 were waited for; matrix products, arithmetic and copies ran while one was open for 9% of the time, Pallas kernels for 0%

commit v1 on v0

--- a/solution.py
+++ b/solution.py
@@ -1,6 +1,10 @@
+import functools
+
 import jax
 import jax.numpy as jnp
 from jax import lax
+from jax.experimental import pallas as pl
+from jax.experimental.pallas import tpu as pltpu
 from jax.sharding import PartitionSpec as P
 
 RESP_LEN = 384
@@ -64,6 +68,104 @@
         + weight_decay * current
     )
     return ((current - learn_rate * update).astype(jnp.bfloat16), new_first, new_second)
+
+
+def update_kernel(place, left, right, weight, first, second, *rest):
+    updated, new_first, new_second = rest[-3:]
+    gradient = jnp.dot(left[...], right[...], preferred_element_type=jnp.float32)
+    updated[...], new_first[...], new_second[...] = adam_rows(
+        weight[...], first[...], second[...], gradient
+    )
+
+
+def update_rows(place, left, right, weight, first, second, carried, start, rows, tile):
+    columns = weight.shape[1]
+    tokens = right.shape[0]
+    tiles = rows // tile
+    begin = start // tile
+    shard_tiles = first.shape[0] // tile
+    here = lambda i, place: (begin + i, 0)
+    moment = pl.BlockSpec((tile, columns), here)
+    in_specs = [
+        pl.BlockSpec((tile, tokens), here),
+        pl.BlockSpec((tokens, columns), lambda i, place: (0, 0)),
+        pl.BlockSpec((tile, columns), lambda i, place: (place[0] * shard_tiles + begin + i, 0)),
+        moment,
+        moment,
+    ]
+    operands = [left, right, weight, first, second]
+    aliases = {}
+    if carried is not None:
+        in_specs += [pl.BlockSpec(memory_space=pl.ANY)] * 2
+        operands += list(carried)
+        aliases = {6: 1, 7: 2}
+    return pl.pallas_call(
+        update_kernel,
+        grid_spec=pltpu.PrefetchScalarGridSpec(
+            num_scalar_prefetch=1,
+            grid=(tiles,),
+            in_specs=in_specs,
+            out_specs=[pl.BlockSpec((tile, columns), lambda i, place: (i, 0)), moment, moment],
+        ),
+        out_shape=[
+            jax.ShapeDtypeStruct((rows, columns), jnp.bfloat16),
+            jax.ShapeDtypeStruct(first.shape, jnp.float32),
+            jax.ShapeDtypeStruct(second.shape, jnp.float32),
+        ],
+        input_output_aliases=aliases,
+        compiler_params=pltpu.CompilerParams(vmem_limit_bytes=40 * 2**20),
+        cost_estimate=pl.CostEstimate(
+            flops=2 * rows * tokens * columns,
+            bytes_accessed=20 * rows * columns,
+            transcendentals=rows * columns,
+        ),
+    )(place, *operands)
+
+
+def place_kernel(count, shard_rows, start, owners, *rest):
+    pieces = rest[:count]
+    sems = rest[-1]
+    whole = rest[-2]
+    rows = pieces[0].shape[0]
+    copies = []
+    for i in range(count):
+        row = pl.multiple_of(owners[i] * shard_rows + start, 16)
+        copies.append(pltpu.make_async_copy(pieces[i], whole.at[pl.ds(row, rows)], sems.at[i]))
+    for copy in copies:
+        copy.start()
+    for copy in copies:
+        copy.wait()
+
+
+def place_rows(owners, pieces, carried, shard_rows, start):
+    count = len(pieces)
+    rows, columns = pieces[0].shape
+    anywhere = pl.BlockSpec(memory_space=pl.ANY)
+    operands = list(pieces) + ([] if carried is None else [carried])
+    return pl.pallas_call(
+        functools.partial(place_kernel, count, shard_rows, start),
+        in_specs=[pl.BlockSpec(memory_space=pltpu.SMEM)] + [anywhere] * len(operands),
+        out_specs=anywhere,
+        out_shape=jax.ShapeDtypeStruct((count * shard_rows, columns), jnp.bfloat16),
+        scratch_shapes=[pltpu.SemaphoreType.DMA((count,))],
+        input_output_aliases={} if carried is None else {count + 1: 0},
+        cost_estimate=pl.CostEstimate(
+            flops=0, bytes_accessed=4 * count * rows * columns, transcendentals=0
+        ),
+    )(owners, *operands)
+
+
+def spread(chunk, me, count):
+    pieces = [(me, chunk)]
+    stride = 2 if count % 2 == 0 else 1
+    for hop in range(stride, count, stride):
+        sent = lax.ppermute(chunk, "dp", [(i, (i + hop) % count) for i in range(count)])
+        pieces.append((lax.rem(me - hop + count, count), sent))
+    if stride == 2:
+        swap = [(i, i ^ 1) for i in range(count)]
+        for owner, piece in list(pieces):
+            pieces.append((owner ^ 1, lax.ppermute(piece, "dp", swap)))
+    return pieces
 
 
 def on_device(
@@ -79,31 +181,73 @@
     first_moment,
     second_moment,
 ):
+    count = lax.axis_size("dp")
+    me = lax.axis_index("dp")
+    shard_rows = first_moment.shape[1]
+    shifts = [[(i, (i + hop) % count) for i in range(count)] for hop in range(1, count)]
+
     gathered = lax.all_gather(activations, "section", axis=0, tiled=True)
     tok_rep = gathered.shape[0]
+    tokens = count * tok_rep
+    blocks = gathered.reshape(tok_rep, count, shard_rows)
+
+    def block_for(owner):
+        return lax.dynamic_index_in_dim(blocks, owner, axis=1, keepdims=False)
+
+    left = [block_for(me)]
+    right = [readout]
+    for hop in range(1, count):
+        left.append(lax.ppermute(block_for(lax.rem(me + hop, count)), "dp", shifts[hop - 1]))
+        right.append(lax.ppermute(readout, "dp", shifts[hop - 1]))
+    order = [lax.rem(me - hop + count, count) for hop in range(count)]
+
     layer_out = jnp.dot(gathered, weight, preferred_element_type=jnp.float32)
     score_share = jnp.sum(layer_out * readout.astype(jnp.float32), axis=1)
-    score = lax.psum(score_share, ("section", "mp"))
-    new_logp = logp_rest + score
-    positions = lax.axis_index("dp") * tok_rep + jnp.arange(tok_rep, dtype=jnp.int32)
+    first_holder = (lax.axis_index("section") + lax.axis_index("mp")) == 0
+    once = jnp.where(first_holder, 1.0, 0.0).astype(jnp.float32)
+    mine = jnp.stack([score_share + once * logp_rest, once * old_logp, once * ref_logp])
+    slots = (jnp.arange(count) == me).astype(jnp.float32)
+    known = lax.psum(mine[:, None, :] * slots[None, :, None], ("section", "dp", "mp"))
+    known = known.reshape(3, tokens)
+    positions = jnp.arange(tokens, dtype=jnp.int32)
     adv_token, token_weight = token_terms(lengths, group_ids, rewards, positions, RESP_LEN)
-    coeff = token_coeff(new_logp, old_logp, ref_logp, adv_token, token_weight)
-    weighted = (coeff[:, None] * readout.astype(jnp.float32)).astype(jnp.bfloat16)
-    shard_rows = first_moment.shape[1]
-    owned = lax.all_to_all(gathered, "dp", split_axis=1, concat_axis=0, tiled=True)
-    piece = lax.all_gather(weighted, "dp", axis=0, tiled=True)
-    count = piece.shape[0]
-    replicas = count // tok_rep
-    left = owned.reshape(replicas, tok_rep, owned.shape[1])
-    right = piece.reshape(replicas, tok_rep, piece.shape[1])
-    parts = jnp.einsum("rts,rtd->rsd", left, right, preferred_element_type=jnp.float32)
-    gradient = jnp.sum(parts.astype(jnp.bfloat16).astype(jnp.float32), axis=0)
-    weight_rows = lax.dynamic_slice_in_dim(weight, lax.axis_index("dp") * shard_rows, shard_rows, 0)
-    updated_rows, new_first, new_second = adam_rows(
-        weight_rows, first_moment[0], second_moment[0], gradient
-    )
-    new_weight = lax.all_gather(updated_rows, "dp", axis=0, tiled=True)
-    return (new_weight, new_first[None], new_second[None])
+    coeff = token_coeff(known[0], known[1], known[2], adv_token, token_weight)
+    coeff = coeff.reshape(count, tok_rep)
+    coeff = jnp.concatenate(
+        [lax.dynamic_index_in_dim(coeff, owner, axis=0, keepdims=False) for owner in order]
+    )
+
+    left = jnp.concatenate(left, axis=0).T
+    right = jnp.concatenate(right, axis=0)
+    weighted = (coeff[:, None] * right.astype(jnp.float32)).astype(jnp.bfloat16)
+
+    chunks = max(n for n in range(1, 7) if shard_rows % (16 * n) == 0)
+    rows = shard_rows // chunks
+    tile = rows // 2 if rows % 32 == 0 else rows
+    where_am_i = me.reshape(1).astype(jnp.int32)
+    moments = None
+    sent = []
+    for chunk in range(chunks):
+        updated, *moments = update_rows(
+            where_am_i,
+            left,
+            weighted,
+            weight,
+            first_moment[0],
+            second_moment[0],
+            moments,
+            chunk * rows,
+            rows,
+            tile,
+        )
+        sent.append(spread(updated, me, count))
+    new_weight = None
+    for chunk, pieces in enumerate(sent):
+        owners = jnp.stack([owner for owner, _ in pieces]).astype(jnp.int32)
+        new_weight = place_rows(
+            owners, [piece for _, piece in pieces], new_weight, shard_rows, chunk * rows
+        )
+    return (new_weight, moments[0][None], moments[1][None])
 
 
 def solution(mesh):

time: 444 us -> 1430 us (3.22)
  Pallas kernels: 0 us -> 1130 us
  waiting for transfers between devices: 266 us -> 191 us
  other arithmetic: 68.1 us -> 10.1 us
  matrix products: 39.2 us -> 15.5 us
  blocking collectives: 16.8 us -> 38.1 us
    pallas_call x0 -> x12, Pallas kernels: none -> 1130 us  [the longest x6 1080 us: place_rows(): pl.pallas_call(functools.partial(place_kernel, count, shard_rows, start),...]
    all_gather x2 -> x0, waiting for transfers between devices: 178 us -> none  [the longest x1 178 us: on_device(): new_weight = lax.all_gather(updated_rows, 'dp', axis=0, tiled=True)]
    ppermute x0 -> x24, waiting for transfers between devices: none -> 154 us  [the longest x6 150 us: spread(): lax.ppermute(chunk, 'dp', [(i, (i + hop) % count) for i in range(count)])]
    all_to_all x1 -> x0, waiting for transfers between devices: 47.1 us -> none  [on_device(): lax.all_to_all(gathered, 'dp', split_axis=1, concat_axis=0, tiled=True)]
    add x1, other arithmetic: 36.4 us -> 0.01 us  [on_device(): score_share + once * logp_rest]
    convert_element_type x2, other arithmetic: 28.3 us -> 3.64 us  [the longest x1 3.63 us: on_device(): weighted = (coeff[:, None] * right.astype(jnp.float32)).astype(jnp.bfloat16)]
    dot_general x1 -> x0, matrix products: 23.5 us -> none  [on_device(): jnp.einsum('rts,rtd->rsd', left, right, preferred_element_type=jnp.float32)]
    psum x1, blocking collectives: 16.8 us -> 38.1 us  [on_device(): lax.psum(mine[:, None, :] * slots[None, :, None], ('section', 'dp', 'mp'))]
  transfers between devices with their start and end apart: 4 -> 25, of which waited for: 3 -> 8; matrix products, arithmetic and copies ran while one was open for 9% -> 3% of each run, Pallas kernels for 0% -> 66%
where the time goes in v1:
time: 1430 us
  Pallas kernels  1130 us (79%)
  waiting for transfers between devices  191 us (13%)
  blocking collectives  38.1 us (3%)
  local copies, waits for them, and re-layouts  25 us (2%)
  matrix products  15.5 us (1%)
  between operations  14.4 us (1%)
    pallas_call x6, Pallas kernels, place_rows(): pl.pallas_call(functools.partial(place_kernel, count, shard_rows, start),...  1080 us
    ppermute x6, waiting for transfers between devices, spread(): lax.ppermute(chunk, 'dp', [(i, (i + hop) % count) for i in range(count)])  150 us
    pallas_call x6, Pallas kernels, update_rows(): pl.pallas_call(update_kernel, grid_spec=pltpu.PrefetchScalarGridSpec(num_...  43.3 us
    psum x1, blocking collectives, on_device(): lax.psum(mine[:, None, :] * slots[None, :, None], ('section', 'dp', 'mp'))  38.1 us
    all_gather x1, waiting for transfers between devices, on_device(): gathered = lax.all_gather(activations, 'section', axis=0, tiled=True)  35.9 us
  transfers between devices with their start and end apart: 25, of which 8 were waited for; matrix products, arithmetic and copies ran while one was open for 3% of the time, Pallas kernels for 66%

profile of v1, /device:TPU:1, one launch (start us, length us, event | category | flops | bytes accessed | tf_op | source)
XLA Modules:
  0.0 1432.6 jit_solution(16964296294108459089)
XLA Ops:
  7.9 2.7 collective-permute-start.3
  15.2 35.9 %all-gather.2.cloned.1.call-done = bf16[192,6912]{1,0:T(8,128)(2,1)} async-done(((bf16[96,6912]{1,0:T(8,128)(2,1)}), bf16[192,6912]{1,0:T(8,128)(2,1)}) %all-gather.2.cloned.1.call-update) | async-done | bytes 2654224 | tf_op jit(solution)/shard_map/all_gather | solution.py:189
  51.1 6.1 reshape.58
  57.1 6.5 constant_dynamic-slice_fusion.7
  64.6 1.7 collective-permute-start
  68.4 1.7 copy.47
  70.2 15.5 %fusion = f32[192]{0:T(256)S(1)} fusion(bf16[192,2560]{1,0:T(8,128)(2,1)S(1)} %copy-done.18, bf16[192,6912]{1,0:T(8,128)(2,1)} %all-gather.2.cloned.1.call-done, bf16[6912,2560]{1,0:T(8,128)(2,1)} %weight.11), kind=kOutput, calls=%fused_computation.3 | convolution fusion | flops 6796247040 | bytes 39027456 | tf_op jit(solution)/shard_map/dot_general | solution.py:204
  85.8 38.1 %psum.7 = f32[3,4,192]{2,1,0:T(4,128)S(1)} all-reduce(f32[3,4,192]{2,1,0:T(4,128)S(1)} %broadcast_multiply_fusion), channel_id=1, replica_groups=mesh['section'=2,'dp'=4,'mp'=4] {'section','dp','mp'}, use_global_device_ids=true, to_apply=%region_2.3 | all-reduce | flops 2304 | bytes 18432 | tf_op jit(solution)/shard_map/psum | solution.py:210
  124.1 1.7 collective-permute-start.2
  125.8 3.6 multiply_convert_fusion.right
  129.4 1.4 copy.44
  130.8 1.4 copy.45
  132.2 4.4 collective-permute-done.2
  138.0 1.7 maximum_bitcast_fusion.left
  140.1 6.9 shard_map.130
  147.3 7.2 shard_map.131
  156.3 6.9 shard_map.132
  163.4 7.3 shard_map.133
  170.7 10.7 collective-permute-done.21.rest_1_
  182.1 30.9 %collective-permute-done.18.rest_1_ = bf16[288,2560]{1,0:T(8,128)(2,1)S(1)} collective-permute-done((bf16[288,2560]{1,0:T(8,128)(2,1)S(1)}, bf16[288,2560]{1,0:T(8,128)(2,1)S(1)}, u32[]{:S(2)}, u32[]{:S(2)}) %collective-permute-start.18) | collective-permute-done | bytes 1474592 | tf_op jit(solution)/shard_map/ppermute | solution.py:162
  213.0 7.7 shard_map.134
  220.7 7.2 shard_map.135
  228.1 16.6 %collective-permute-done.15.rest_1_ = bf16[288,2560]{1,0:T(8,128)(2,1)S(1)} collective-permute-done((bf16[288,2560]{1,0:T(8,128)(2,1)S(1)}, bf16[288,2560]{1,0:T(8,128)(2,1)S(1)}, u32[]{:S(2)}, u32[]{:S(2)}) %collective-permute-start.15) | collective-permute-done | bytes 1474592 | tf_op jit(solution)/shard_map/ppermute | solution.py:162
  245.6 30.7 %collective-permute-done.12.rest_1_ = bf16[288,2560]{1,0:T(8,128)(2,1)} collective-permute-done((bf16[288,2560]{1,0:T(8,128)(2,1)S(1)}, bf16[288,2560]{1,0:T(8,128)(2,1)}, u32[]{:S(2)}, u32[]{:S(2)}) %collective-permute-start.12) | collective-permute-done | bytes 1474592 | tf_op jit(solution)/shard_map/ppermute | solution.py:162
  276.8 31.1 %collective-permute-done.9.rest_1_ = bf16[288,2560]{1,0:T(8,128)(2,1)} collective-permute-done((bf16[288,2560]{1,0:T(8,128)(2,1)}, bf16[288,2560]{1,0:T(8,128)(2,1)}, u32[]{:S(2)}, u32[]{:S(2)}) %collective-permute-start.9) | collective-permute-done | bytes 1474592 | tf_op jit(solution)/shard_map/ppermute | solution.py:162
  307.9 29.9 %collective-permute-done.6.rest_1_ = bf16[288,2560]{1,0:T(8,128)(2,1)} collective-permute-done((bf16[288,2560]{1,0:T(8,128)(2,1)S(1)}, bf16[288,2560]{1,0:T(8,128)(2,1)}, u32[]{:S(2)}, u32[]{:S(2)}) %collective-permute-start.6) | collective-permute-done | bytes 1474592 | tf_op jit(solution)/shard_map/ppermute | solution.py:162
  341.6 180.5 %shard_map.136.rest_4_ = bf16[6912,2560]{1,0:T(8,128)(2,1)} custom-call(s32[4]{0:T(128)} %pad_add_fusion.owners, bf16[288,2560]{1,0:T(8,128)(2,1)} %copy-done.1, bf16[288,2560]{1,0:T(8,128)(2,1)} %copy-done.7, bf16[288,2560]{1,0:T(8,128)(2,1)} %copy-done.8, bf16[288,2560]{1,0:T(8,128)(2,1)} %copy-done.15), custom_call_target="tpu_custom_call" | custom-call | bytes 11796480 | tf_op jit(solution)/shard_map/pallas_call | solution.py:145
  522.1 180.5 %shard_map.137.rest_4_ = bf16[6912,2560]{1,0:T(8,128)(2,1)} custom-call(s32[4]{0:T(128)} %pad_add_fusion.owners, bf16[288,2560]{1,0:T(8,128)(2,1)} %copy-done.2, bf16[288,2560]{1,0:T(8,128)(2,1)} %copy-done.9, bf16[288,2560]{1,0:T(8,128)(2,1)} %copy-done.10, bf16[288,2560]{1,0:T(8,128)(2,1)} %copy-done.16, ...), custom_call_target="tpu_custom_call", output_to_operand_aliasing={{}: (5, {})} | custom-call | bytes 11796480 | tf_op jit(solution)/shard_map/pallas_call | solution.py:145
  702.6 180.5 %shard_map.138.rest_4_ = bf16[6912,2560]{1,0:T(8,128)(2,1)} custom-call(s32[4]{0:T(128)} %pad_add_fusion.owners, bf16[288,2560]{1,0:T(8,128)(2,1)} %copy-done.3, bf16[288,2560]{1,0:T(8,128)(2,1)} %copy-done.11, bf16[288,2560]{1,0:T(8,128)(2,1)} %copy-done.12, bf16[288,2560]{1,0:T(8,128)(2,1)} %copy-done.17, ...), custom_call_target="tpu_custom_call", output_to_operand_aliasing={{}: (5, {})} | custom-call | bytes 11796480 | tf_op jit(solution)/shard_map/pallas_call | solution.py:145
  883.1 180.5 %shard_map.139.rest_4_ = bf16[6912,2560]{1,0:T(8,128)(2,1)} custom-call(s32[4]{0:T(128)} %pad_add_fusion.owners, bf16[288,2560]{1,0:T(8,128)(2,1)} %copy-done.4, bf16[288,2560]{1,0:T(8,128)(2,1)} %collective-permute-done.12.rest_1_, bf16[288,2560]{1,0:T(8,128)(2,1)} %copy-done.13, ...), custom_call_target="tpu_custom_call", output_to_operand_aliasing={{}: (5, {})} | custom-call | bytes 11796480 | tf_op jit(solution)/shard_map/pallas_call | solution.py:145
  1063.6 180.5 %shard_map.140.rest_4_ = bf16[6912,2560]{1,0:T(8,128)(2,1)} custom-call(s32[4]{0:T(128)} %pad_add_fusion.owners, bf16[288,2560]{1,0:T(8,128)(2,1)} %get-tuple-element.32.rest_0_, bf16[288,2560]{1,0:T(8,128)(2,1)} %collective-permute-done.9.rest_1_, bf16[288,2560]{1,0:T(8,128)(2,1)} %collective-permute-done.10.rest_2_, ...), custom_call_target="tpu_custom_call", output_to_operand_aliasing={{}: (5, {})} | custom-call | bytes 11796480 | tf_op jit(solution)/shard_map/pallas_call | solution.py:145
  1245.2 180.5 %shard_map.141 = bf16[6912,2560]{1,0:T(8,128)(2,1)} custom-call(s32[4]{0:T(128)} %pad_add_fusion.owners, bf16[288,2560]{1,0:T(8,128)(2,1)} %copy-done.5, bf16[288,2560]{1,0:T(8,128)(2,1)} %collective-permute-done.6.rest_1_, bf16[288,2560]{1,0:T(8,128)(2,1)} %copy-done.14, ...), custom_call_target="tpu_custom_call", output_to_operand_aliasing={{}: (5, {})} | custom-call | bytes 11796480 | tf_op jit(solution)/shard_map/pallas_call | solution.py:145
  (102 shorter events, 19.8 us)
Async XLA Ops:
  7.2 43.9 %all-gather.2.cloned.1.call-start = ((), (), s32[]{:S(2)}) async-start(), calls=%async_computation | async-start | bytes 3981312 | tf_op jit(solution)/shard_map/all_gather | solution.py:189
  7.9 116.2 %collective-permute-start.3 = (bf16[192,2560]{1,0:T(8,128)(2,1)}, bf16[192,2560]{1,0:T(8,128)(2,1)}, u32[]{:S(2)}, u32[]{:S(2)}) collective-permute-start(bf16[192,2560]{1,0:T(8,128)(2,1)} %param.13), channel_id=1, source_target_pairs={{0,4},{4,8},{8,12},{12,0},{1,5},{5,9},{9,13},{13,1},{2,6},{6,10},{... | collective-permute-start | bytes 2949128 | tf_op jit(solution)/shard_map/ppermute | solution.py:201
  10.6 115.2 %collective-permute-start.4 = (bf16[192,2560]{1,0:T(8,128)(2,1)}, bf16[192,2560]{1,0:T(8,128)(2,1)}, u32[]{:S(2)}, u32[]{:S(2)}) collective-permute-start(bf16[192,2560]{1,0:T(8,128)(2,1)} %param.13), channel_id=1, source_target_pairs={{0,8},{4,12},{8,0},{12,4},{1,9},{5,13},{9,1},{13,5},{2,10},{6,14},... | collective-permute-start | bytes 2949128 | tf_op jit(solution)/shard_map/ppermute | solution.py:201
  10.6 115.2 %collective-permute-start.5 = (bf16[192,2560]{1,0:T(8,128)(2,1)}, bf16[192,2560]{1,0:T(8,128)(2,1)}, u32[]{:S(2)}, u32[]{:S(2)}) collective-permute-start(bf16[192,2560]{1,0:T(8,128)(2,1)} %param.13), channel_id=1, source_target_pairs={{0,12},{4,0},{8,4},{12,8},{1,13},{5,1},{9,5},{13,9},{2,14},{6,2},{... | collective-permute-start | bytes 2949128 | tf_op jit(solution)/shard_map/ppermute | solution.py:201
  64.6 64.8 %collective-permute-start = (bf16[192,1728]{1,0:T(8,128)(2,1)}, bf16[192,1728]{1,0:T(8,128)(2,1)}, u32[]{:S(2)}, u32[]{:S(2)}) collective-permute-start(bf16[192,1728]{1,0:T(8,128)(2,1)} %bitcast.42), channel_id=1, source_target_pairs={{0,4},{4,8},{8,12},{12,0},{1,5},{5,9},{9,13},{13,1},{2,6},{6,10},{... | collective-permute-start | bytes 1990664 | tf_op jit(solution)/shard_map/ppermute | solution.py:200
  67.2 63.6 %collective-permute-start.1 = (bf16[192,1728]{1,0:T(8,128)(2,1)}, bf16[192,1728]{1,0:T(8,128)(2,1)}, u32[]{:S(2)}, u32[]{:S(2)}) collective-permute-start(bf16[192,1728]{1,0:T(8,128)(2,1)} %bitcast.41), channel_id=1, source_target_pairs={{0,8},{4,12},{8,0},{12,4},{1,9},{5,13},{9,1},{13,5},{2,10},{6,14},... | collective-permute-start | bytes 1990664 | tf_op jit(solution)/shard_map/ppermute | solution.py:200
  124.1 12.5 collective-permute-start.2
  147.0 34.3 %collective-permute-start.21 = (bf16[288,2560]{1,0:T(8,128)(2,1)S(1)}, bf16[288,2560]{1,0:T(8,128)(2,1)S(1)}, u32[]{:S(2)}, u32[]{:S(2)}) collective-permute-start(bf16[288,2560]{1,0:T(8,128)(2,1)S(1)} %get-tuple-element.36.rest_0_), channel_id=1, source_target_pairs={{0,8},{4,12},{8,0},{12,4},{1,9},{5,13},{9,1},{13,5},{2,10},{6,14},... | collective-permute-start | bytes 4423688 | tf_op jit(solution)/shard_map/ppermute | solution.py:162
  147.1 34.4 %collective-permute-start.22 = (bf16[288,2560]{1,0:T(8,128)(2,1)S(1)}, bf16[288,2560]{1,0:T(8,128)(2,1)S(1)}, u32[]{:S(2)}, u32[]{:S(2)}) collective-permute-start(bf16[288,2560]{1,0:T(8,128)(2,1)S(1)} %get-tuple-element.36.rest_0_), channel_id=1, source_target_pairs={{0,4},{4,0},{8,12},{12,8},{1,5},{5,1},{9,13},{13,9},{2,6},{6,2},{1... | collective-permute-start | bytes 4423688 | tf_op jit(solution)/shard_map/ppermute | solution.py:167
  154.5 58.5 %collective-permute-start.18 = (bf16[288,2560]{1,0:T(8,128)(2,1)S(1)}, bf16[288,2560]{1,0:T(8,128)(2,1)S(1)}, u32[]{:S(2)}, u32[]{:S(2)}) collective-permute-start(bf16[288,2560]{1,0:T(8,128)(2,1)S(1)} %get-tuple-element.35.rest_0_), channel_id=1, source_target_pairs={{0,8},{4,12},{8,0},{12,4},{1,9},{5,13},{9,1},{13,5},{2,10},{6,14},... | collective-permute-start | bytes 4423688 | tf_op jit(solution)/shard_map/ppermute | solution.py:162
  155.5 72.4 %collective-permute-start.19 = (bf16[288,2560]{1,0:T(8,128)(2,1)S(1)}, bf16[288,2560]{1,0:T(8,128)(2,1)S(1)}, u32[]{:S(2)}, u32[]{:S(2)}) collective-permute-start(bf16[288,2560]{1,0:T(8,128)(2,1)S(1)} %get-tuple-element.35.rest_0_), channel_id=1, source_target_pairs={{0,4},{4,0},{8,12},{12,8},{1,5},{5,1},{9,13},{13,9},{2,6},{6,2},{1... | collective-permute-start | bytes 4423688 | tf_op jit(solution)/shard_map/ppermute | solution.py:167
  163.2 81.5 %collective-permute-start.15 = (bf16[288,2560]{1,0:T(8,128)(2,1)S(1)}, bf16[288,2560]{1,0:T(8,128)(2,1)S(1)}, u32[]{:S(2)}, u32[]{:S(2)}) collective-permute-start(bf16[288,2560]{1,0:T(8,128)(2,1)S(1)} %get-tuple-element.34.rest_0_), channel_id=1, source_target_pairs={{0,8},{4,12},{8,0},{12,4},{1,9},{5,13},{9,1},{13,5},{2,10},{6,14},... | collective-permute-start | bytes 4423688 | tf_op jit(solution)/shard_map/ppermute | solution.py:162
  181.4 63.3 %copy-start.7 = (bf16[288,2560]{1,0:T(8,128)(2,1)}, bf16[288,2560]{1,0:T(8,128)(2,1)S(1)}, u32[]{:S(2)}) copy-start(bf16[288,2560]{1,0:T(8,128)(2,1)S(1)} %collective-permute-done.21.rest_1_) | copy-start | bytes 4423684
  181.4 63.3 %collective-permute-start.16 = (bf16[288,2560]{1,0:T(8,128)(2,1)S(1)}, bf16[288,2560]{1,0:T(8,128)(2,1)S(1)}, u32[]{:S(2)}, u32[]{:S(2)}) collective-permute-start(bf16[288,2560]{1,0:T(8,128)(2,1)S(1)} %get-tuple-element.34.rest_0_), channel_id=1, source_target_pairs={{0,4},{4,0},{8,12},{12,8},{1,5},{5,1},{9,13},{13,9},{2,6},{6,2},{1... | collective-permute-start | bytes 4423688 | tf_op jit(solution)/shard_map/ppermute | solution.py:167
  181.4 94.9 %collective-permute-start.12 = (bf16[288,2560]{1,0:T(8,128)(2,1)S(1)}, bf16[288,2560]{1,0:T(8,128)(2,1)}, u32[]{:S(2)}, u32[]{:S(2)}) collective-permute-start(bf16[288,2560]{1,0:T(8,128)(2,1)S(1)} %get-tuple-element.33.rest_0_), channel_id=1, source_target_pairs={{0,8},{4,12},{8,0},{12,4},{1,9},{5,13},{9,1},{13,5},{2,10},{6,14},... | collective-permute-start | bytes 4423688 | tf_op jit(solution)/shard_map/ppermute | solution.py:162
  213.0 63.3 %copy-start.9 = (bf16[288,2560]{1,0:T(8,128)(2,1)}, bf16[288,2560]{1,0:T(8,128)(2,1)S(1)}, u32[]{:S(2)}) copy-start(bf16[288,2560]{1,0:T(8,128)(2,1)S(1)} %collective-permute-done.18.rest_1_) | copy-start | bytes 4423684
  213.0 63.3 %collective-permute-start.13 = (bf16[288,2560]{1,0:T(8,128)(2,1)S(1)}, bf16[288,2560]{1,0:T(8,128)(2,1)S(1)}, u32[]{:S(2)}, u32[]{:S(2)}) collective-permute-start(bf16[288,2560]{1,0:T(8,128)(2,1)S(1)} %get-tuple-element.33.rest_0_), channel_id=1, source_target_pairs={{0,4},{4,0},{8,12},{12,8},{1,5},{5,1},{9,13},{13,9},{2,6},{6,2},{1... | collective-permute-start | bytes 4423688 | tf_op jit(solution)/shard_map/ppermute | solution.py:167
  227.9 294.2 %copy-start.5 = (bf16[288,2560]{1,0:T(8,128)(2,1)}, bf16[288,2560]{1,0:T(8,128)(2,1)S(1)}, u32[]{:S(2)}) copy-start(bf16[288,2560]{1,0:T(8,128)(2,1)S(1)} %get-tuple-element.31.rest_0_) | copy-start | bytes 4423684
  227.9 110.5 %copy-start.10 = (bf16[288,2560]{1,0:T(8,128)(2,1)}, bf16[288,2560]{1,0:T(8,128)(2,1)S(1)}, u32[]{:S(2)}) copy-start(bf16[288,2560]{1,0:T(8,128)(2,1)S(1)} %collective-permute-done.19.rest_2_) | copy-start | bytes 4423684
  227.9 80.0 %collective-permute-start.9 = (bf16[288,2560]{1,0:T(8,128)(2,1)}, bf16[288,2560]{1,0:T(8,128)(2,1)}, u32[]{:S(2)}, u32[]{:S(2)}) collective-permute-start(bf16[288,2560]{1,0:T(8,128)(2,1)} %get-tuple-element.32.rest_0_), channel_id=1, source_target_pairs={{0,8},{4,12},{8,0},{12,4},{1,9},{5,13},{9,1},{13,5},{2,10},{6,14},... | collective-permute-start | bytes 4423688 | tf_op jit(solution)/shard_map/ppermute | solution.py:162
  244.7 93.8 %copy-start.11 = (bf16[288,2560]{1,0:T(8,128)(2,1)}, bf16[288,2560]{1,0:T(8,128)(2,1)S(1)}, u32[]{:S(2)}) copy-start(bf16[288,2560]{1,0:T(8,128)(2,1)S(1)} %collective-permute-done.15.rest_1_) | copy-start | bytes 4423684
  244.7 93.1 %collective-permute-start.6 = (bf16[288,2560]{1,0:T(8,128)(2,1)S(1)}, bf16[288,2560]{1,0:T(8,128)(2,1)}, u32[]{:S(2)}, u32[]{:S(2)}) collective-permute-start(bf16[288,2560]{1,0:T(8,128)(2,1)S(1)} %get-tuple-element.31.rest_0_), channel_id=1, source_target_pairs={{0,8},{4,12},{8,0},{12,4},{1,9},{5,13},{9,1},{13,5},{2,10},{6,14},... | collective-permute-start | bytes 4423688 | tf_op jit(solution)/shard_map/ppermute | solution.py:162
  244.7 93.8 %copy-start.12 = (bf16[288,2560]{1,0:T(8,128)(2,1)}, bf16[288,2560]{1,0:T(8,128)(2,1)S(1)}, u32[]{:S(2)}) copy-start(bf16[288,2560]{1,0:T(8,128)(2,1)S(1)} %collective-permute-done.16.rest_2_) | copy-start | bytes 4423684
  244.7 93.1 %collective-permute-start.23 = (bf16[288,2560]{1,0:T(8,128)(2,1)S(1)}, bf16[288,2560]{1,0:T(8,128)(2,1)S(1)}, u32[]{:S(2)}, u32[]{:S(2)}) collective-permute-start(bf16[288,2560]{1,0:T(8,128)(2,1)S(1)} %collective-permute-done.21.rest_1_), channel_id=1, source_target_pairs={{0,4},{4,0},{8,12},{12,8},{1,5},{5,1},{9,13},{13,9},{2,6},{6,2},{1... | collective-permute-start | bytes 4423688 | tf_op jit(solution)/shard_map/ppermute | solution.py:167
  276.3 62.0 %collective-permute-start.20 = (bf16[288,2560]{1,0:T(8,128)(2,1)S(1)}, bf16[288,2560]{1,0:T(8,128)(2,1)S(1)}, u32[]{:S(2)}, u32[]{:S(2)}) collective-permute-start(bf16[288,2560]{1,0:T(8,128)(2,1)S(1)} %collective-permute-done.18.rest_1_), channel_id=1, source_target_pairs={{0,4},{4,0},{8,12},{12,8},{1,5},{5,1},{9,13},{13,9},{2,6},{6,2},{1... | collective-permute-start | bytes 4423688 | tf_op jit(solution)/shard_map/ppermute | solution.py:167
  276.3 62.2 %copy-start.13 = (bf16[288,2560]{1,0:T(8,128)(2,1)}, bf16[288,2560]{1,0:T(8,128)(2,1)S(1)}, u32[]{:S(2)}) copy-start(bf16[288,2560]{1,0:T(8,128)(2,1)S(1)} %collective-permute-done.13.rest_2_) | copy-start | bytes 4423684
  276.3 62.2 %collective-permute-start.17 = (bf16[288,2560]{1,0:T(8,128)(2,1)S(1)}, bf16[288,2560]{1,0:T(8,128)(2,1)S(1)}, u32[]{:S(2)}, u32[]{:S(2)}) collective-permute-start(bf16[288,2560]{1,0:T(8,128)(2,1)S(1)} %collective-permute-done.15.rest_1_), channel_id=1, source_target_pairs={{0,4},{4,0},{8,12},{12,8},{1,5},{5,1},{9,13},{13,9},{2,6},{6,2},{1... | collective-permute-start | bytes 4423688 | tf_op jit(solution)/shard_map/ppermute | solution.py:167
  307.9 755.7 %collective-permute-start.10 = (bf16[288,2560]{1,0:T(8,128)(2,1)}, bf16[288,2560]{1,0:T(8,128)(2,1)}, u32[]{:S(2)}, u32[]{:S(2)}) collective-permute-start(bf16[288,2560]{1,0:T(8,128)(2,1)} %get-tuple-element.32.rest_0_), channel_id=1, source_target_pairs={{0,4},{4,0},{8,12},{12,8},{1,5},{5,1},{9,13},{13,9},{2,6},{6,2},{1... | collective-permute-start | bytes 4423688 | tf_op jit(solution)/shard_map/ppermute | solution.py:167
  337.8 545.3 %collective-permute-start.14 = (bf16[288,2560]{1,0:T(8,128)(2,1)}, bf16[288,2560]{1,0:T(8,128)(2,1)}, u32[]{:S(2)}, u32[]{:S(2)}) collective-permute-start(bf16[288,2560]{1,0:T(8,128)(2,1)} %collective-permute-done.12.rest_1_), channel_id=1, source_target_pairs={{0,4},{4,0},{8,12},{12,8},{1,5},{5,1},{9,13},{13,9},{2,6},{6,2},{1... | collective-permute-start | bytes 4423688 | tf_op jit(solution)/shard_map/ppermute | solution.py:167
  337.8 725.8 %collective-permute-start.11 = (bf16[288,2560]{1,0:T(8,128)(2,1)}, bf16[288,2560]{1,0:T(8,128)(2,1)}, u32[]{:S(2)}, u32[]{:S(2)}) collective-permute-start(bf16[288,2560]{1,0:T(8,128)(2,1)} %collective-permute-done.9.rest_1_), channel_id=1, source_target_pairs={{0,4},{4,0},{8,12},{12,8},{1,5},{5,1},{9,13},{13,9},{2,6},{6,2},{1... | collective-permute-start | bytes 4423688 | tf_op jit(solution)/shard_map/ppermute | solution.py:167
  338.4 905.8 %collective-permute-start.7 = (bf16[288,2560]{1,0:T(8,128)(2,1)S(1)}, bf16[288,2560]{1,0:T(8,128)(2,1)S(1)}, u32[]{:S(2)}, u32[]{:S(2)}) collective-permute-start(bf16[288,2560]{1,0:T(8,128)(2,1)S(1)} %get-tuple-element.31.rest_0_), channel_id=1, source_target_pairs={{0,4},{4,0},{8,12},{12,8},{1,5},{5,1},{9,13},{13,9},{2,6},{6,2},{1... | collective-permute-start | bytes 4423688 | tf_op jit(solution)/shard_map/ppermute | solution.py:167
  340.6 903.5 %collective-permute-start.8 = (bf16[288,2560]{1,0:T(8,128)(2,1)}, bf16[288,2560]{1,0:T(8,128)(2,1)}, u32[]{:S(2)}, u32[]{:S(2)}) collective-permute-start(bf16[288,2560]{1,0:T(8,128)(2,1)} %collective-permute-done.6.rest_1_), channel_id=1, source_target_pairs={{0,4},{4,0},{8,12},{12,8},{1,5},{5,1},{9,13},{13,9},{2,6},{6,2},{1... | collective-permute-start | bytes 4423688 | tf_op jit(solution)/shard_map/ppermute | solution.py:167
  (13 other events, 154.4 us)
Sparse Core Ops, SparseCore 0:
  9.5 41.4 all-gather.1

commit v2 on v1

--- a/solution.py
+++ b/solution.py
@@ -78,7 +78,7 @@
     )
 
 
-def update_rows(place, left, right, weight, first, second, carried, start, rows, tile):
+def update_rows(place, left, right, weight, first, second, carried, after, start, rows, tile):
     columns = weight.shape[1]
     tokens = right.shape[0]
     tiles = rows // tile
@@ -99,6 +99,9 @@
         in_specs += [pl.BlockSpec(memory_space=pl.ANY)] * 2
         operands += list(carried)
         aliases = {6: 1, 7: 2}
+    if after is not None:
+        in_specs.append(pl.BlockSpec(memory_space=pl.ANY))
+        operands.append(after)
     return pl.pallas_call(
         update_kernel,
         grid_spec=pltpu.PrefetchScalarGridSpec(
@@ -124,16 +127,21 @@
 
 def place_kernel(count, shard_rows, start, owners, *rest):
     pieces = rest[:count]
-    sems = rest[-1]
-    whole = rest[-2]
+    whole, token, held, in_sems, out_sems = rest[-5:]
     rows = pieces[0].shape[0]
-    copies = []
+    into = [
+        pltpu.make_async_copy(pieces[i], held.at[i], in_sems.at[i]) for i in range(count)
+    ]
+    for copy in into:
+        copy.start()
+    token[...] = jnp.zeros_like(token)
+    out = []
     for i in range(count):
         row = pl.multiple_of(owners[i] * shard_rows + start, 16)
-        copies.append(pltpu.make_async_copy(pieces[i], whole.at[pl.ds(row, rows)], sems.at[i]))
-    for copy in copies:
-        copy.start()
-    for copy in copies:
+        into[i].wait()
+        out.append(pltpu.make_async_copy(held.at[i], whole.at[pl.ds(row, rows)], out_sems.at[i]))
+        out[i].start()
+    for copy in out:
         copy.wait()
 
 
@@ -145,10 +153,18 @@
     return pl.pallas_call(
         functools.partial(place_kernel, count, shard_rows, start),
         in_specs=[pl.BlockSpec(memory_space=pltpu.SMEM)] + [anywhere] * len(operands),
-        out_specs=anywhere,
-        out_shape=jax.ShapeDtypeStruct((count * shard_rows, columns), jnp.bfloat16),
-        scratch_shapes=[pltpu.SemaphoreType.DMA((count,))],
+        out_specs=[anywhere, pl.BlockSpec(memory_space=pltpu.VMEM)],
+        out_shape=[
+            jax.ShapeDtypeStruct((count * shard_rows, columns), jnp.bfloat16),
+            jax.ShapeDtypeStruct((8, 128), jnp.float32),
+        ],
+        scratch_shapes=[
+            pltpu.VMEM((count, rows, columns), jnp.bfloat16),
+            pltpu.SemaphoreType.DMA((count,)),
+            pltpu.SemaphoreType.DMA((count,)),
+        ],
         input_output_aliases={} if carried is None else {count + 1: 0},
+        compiler_params=pltpu.CompilerParams(vmem_limit_bytes=40 * 2**20),
         cost_estimate=pl.CostEstimate(
             flops=0, bytes_accessed=4 * count * rows * columns, transcendentals=0
         ),
@@ -225,9 +241,21 @@
     rows = shard_rows // chunks
     tile = rows // 2 if rows % 32 == 0 else rows
     where_am_i = me.reshape(1).astype(jnp.int32)
-    moments = None
-    sent = []
+    moments = new_weight = None
+    sent, placed = [], []
+
+    def place(chunk):
+        pieces = sent[chunk]
+        owners = jnp.stack([owner for owner, _ in pieces]).astype(jnp.int32)
+        whole, token = place_rows(
+            owners, [piece for _, piece in pieces], new_weight, shard_rows, chunk * rows
+        )
+        placed.append(token)
+        return whole
+
     for chunk in range(chunks):
+        if chunk >= 2:
+            new_weight = place(chunk - 2)
         updated, *moments = update_rows(
             where_am_i,
             left,
@@ -236,17 +264,14 @@
             first_moment[0],
             second_moment[0],
             moments,
+            placed[-1] if placed else None,
             chunk * rows,
             rows,
             tile,
         )
         sent.append(spread(updated, me, count))
-    new_weight = None
-    for chunk, pieces in enumerate(sent):
-        owners = jnp.stack([owner for owner, _ in pieces]).astype(jnp.int32)
-        new_weight = place_rows(
-            owners, [piece for _, piece in pieces], new_weight, shard_rows, chunk * rows
-        )
+    for chunk in range(max(chunks - 2, 0), chunks):
+        new_weight = place(chunk)
     return (new_weight, moments[0][None], moments[1][None])
 
 

time: 1430 us -> 387 us (0.27)
  Pallas kernels: 1130 us -> 72.3 us
    pallas_call x6, Pallas kernels: 1080 us -> 29.7 us  [place_rows(): pl.pallas_call(functools.partial(place_kernel, count, shard_rows, start),...]
  transfers between devices with their start and end apart: 25 -> 25, of which waited for: 8 -> 8; matrix products, arithmetic and copies ran while one was open for 3% -> 12% of each run, Pallas kernels for 66% -> 16%
where the time goes in v2:
time: 387 us
  waiting for transfers between devices  195 us (50%)
  Pallas kernels  72.3 us (19%)
  blocking collectives  38 us (10%)
  local copies, waits for them, and re-layouts  23.1 us (6%)
  starting transfers between devices  17.3 us (4%)
  matrix products  15.6 us (4%)
  between operations  14.3 us (4%)
  other arithmetic  11.6 us (3%)
    ppermute x6, waiting for transfers between devices, spread(): lax.ppermute(chunk, 'dp', [(i, (i + hop) % count) for i in range(count)])  156 us
    pallas_call x6, Pallas kernels, update_rows(): pl.pallas_call(update_kernel, grid_spec=pltpu.PrefetchScalarGridSpec(num_...  42.7 us
    psum x1, blocking collectives, on_device(): lax.psum(mine[:, None, :] * slots[None, :, None], ('section', 'dp', 'mp'))  38 us
    all_gather x1, waiting for transfers between devices, on_device(): gathered = lax.all_gather(activations, 'section', axis=0, tiled=True)  35.3 us
    pallas_call x6, Pallas kernels, place_rows(): pl.pallas_call(functools.partial(place_kernel, count, shard_rows, start),...  29.7 us
    dot_general x1, matrix products, on_device(): layer_out = jnp.dot(gathered, weight, preferred_element_type=jnp.float32)  15.6 us
  transfers between devices with their start and end apart: 25, of which 8 were waited for; matrix products, arithmetic and copies ran while one was open for 12% of the time, Pallas kernels for 16%

profile of v2, /device:TPU:1, one launch (start us, length us, event | category | flops | bytes accessed | tf_op | source)
XLA Modules:
  0.0 386.7 jit_solution(3466084730131182618)
XLA Ops:
  7.9 2.7 collective-permute-start.3
  15.7 35.3 %all-gather.2.cloned.1.call-done = bf16[192,6912]{1,0:T(8,128)(2,1)} async-done(((bf16[96,6912]{1,0:T(8,128)(2,1)}), bf16[192,6912]{1,0:T(8,128)(2,1)}) %all-gather.2.cloned.1.call-update) | async-done | bytes 2654224 | tf_op jit(solution)/shard_map/all_gather | solution.py:205
  51.1 6.1 %reshape.58 = bf16[192,4,1728]{2,1,0:T(4,128)(2,1)S(1)} reshape(bf16[192,6912]{1,0:T(8,128)(2,1)} %all-gather.2.cloned.1.call-done) | data formatting | bytes 5308416 | tf_op jit(solution)/shard_map/reshape | solution.py:208
  57.1 6.5 %constant_dynamic-slice_fusion.7 = (bf16[192,1,1728]{2,1,0:T(2,128)(2,1)}, bf16[192,1,1728]{2,1,0:T(2,128)(2,1)S(1)}, bf16[192,1,1728]{2,1,0:T(2,128)(2,1)S(1)}, bf16[192,1,1728]{2,1,0:T(2,128)(2,1)S(1)}) fusion(bf16[192,4,1728]{2,1,0:T(4,128)(2,1)S(1)} %reshape.58, s32[]{:T(128)S(6)} %select_n.84, s32[]{:T(128)S(6)} %select_n.85, s32[]{:T(128)S(6)} %select_n.87, ...), kind=kLoop, calls=%fused_computation.50 | loop fusion | bytes 5308432 | tf_op jit(solution)/shard_map/jit(dynamic_index_in_dim)/dynamic_slice | solution.py:211
  64.5 1.7 collective-permute-start
  70.2 15.6 %fusion = f32[192]{0:T(256)S(1)} fusion(bf16[192,2560]{1,0:T(8,128)(2,1)S(1)} %copy-done.3, bf16[192,6912]{1,0:T(8,128)(2,1)} %all-gather.2.cloned.1.call-done, bf16[6912,2560]{1,0:T(8,128)(2,1)} %weight.11), kind=kOutput, calls=%fused_computation.3 | convolution fusion | flops 6796247040 | bytes 39027456 | tf_op jit(solution)/shard_map/dot_general | solution.py:220
  85.9 38.0 %psum.7 = f32[3,4,192]{2,1,0:T(4,128)S(1)} all-reduce(f32[3,4,192]{2,1,0:T(4,128)S(1)} %broadcast_multiply_fusion), channel_id=1, replica_groups=mesh['section'=2,'dp'=4,'mp'=4] {'section','dp','mp'}, use_global_device_ids=true, to_apply=%region_2.3 | all-reduce | flops 2304 | bytes 18432 | tf_op jit(solution)/shard_map/psum | solution.py:226
  124.1 1.7 collective-permute-start.2
  125.8 3.7 multiply_convert_fusion.right
  129.5 2.3 copy.44
  131.8 2.3 copy.45
  134.1 2.2 collective-permute-done.2
  137.5 3.1 maximum_bitcast_fusion.left
  140.7 7.2 %shard_map.130 = (bf16[288,2560]{1,0:T(8,128)(2,1)}, f32[1728,2560]{1,0:T(8,128)}, f32[1728,2560]{1,0:T(8,128)}) custom-call(s32[1]{0:T(128)} %bitcast.place, bf16[1728,768]{1,0:T(8,128)(2,1)S(1)} %maximum_bitcast_fusion.left, bf16[768,2560]{1,0:T(8,128)(2,1)S(1)} %copy-done, bf16[6912,2560]{1,0:T(8,128)(2,1)} %weight.11, f32[1728,2560]{1,0:T(8,128)} %bitcast.43, ...), custom_call_target="tpu_custom_call" | custom-call | flops 1132462080 | bytes 14745600 | tf_op jit(solution)/shard_map/pallas_call | solution.py:105
  147.8 7.2 %shard_map.131 = (bf16[288,2560]{1,0:T(8,128)(2,1)}, f32[1728,2560]{1,0:T(8,128)}, f32[1728,2560]{1,0:T(8,128)}) custom-call(s32[1]{0:T(128)} %bitcast.place, bf16[1728,768]{1,0:T(8,128)(2,1)S(1)} %maximum_bitcast_fusion.left, bf16[768,2560]{1,0:T(8,128)(2,1)S(1)} %copy-done, ...), custom_call_target="tpu_custom_call", output_to_operand_aliasing={{1}: (6, {}), {2}: (7, {})} | custom-call | flops 1132462080 | bytes 14745600 | tf_op jit(solution)/shard_map/pallas_call | solution.py:105
  156.5 26.0 %collective-permute-done.6.rest_1_ = bf16[288,2560]{1,0:T(8,128)(2,1)} collective-permute-done((bf16[288,2560]{1,0:T(8,128)(2,1)}, bf16[288,2560]{1,0:T(8,128)(2,1)}, u32[]{:S(2)}, u32[]{:S(2)}) %collective-permute-start.6) | collective-permute-done | bytes 1474592 | tf_op jit(solution)/shard_map/ppermute | solution.py:178
  183.0 29.4 %collective-permute-done.9.rest_1_ = bf16[288,2560]{1,0:T(8,128)(2,1)} collective-permute-done((bf16[288,2560]{1,0:T(8,128)(2,1)}, bf16[288,2560]{1,0:T(8,128)(2,1)}, u32[]{:S(2)}, u32[]{:S(2)}) %collective-permute-start.9) | collective-permute-done | bytes 1474592 | tf_op jit(solution)/shard_map/ppermute | solution.py:178
  212.5 5.6 %shard_map.132 = (bf16[6912,2560]{1,0:T(8,128)(2,1)}, f32[8,128]{1,0:T(8,128)S(1)}) custom-call(s32[4]{0:T(128)S(1)} %pad_add_fusion.owners, bf16[288,2560]{1,0:T(8,128)(2,1)} %get-tuple-element.35.rest_0_, bf16[288,2560]{1,0:T(8,128)(2,1)} %collective-permute-done.6.rest_1_, bf16[288,2560]{1,0:T(8,128)(2,1)} %collective-permute-done.7.rest_2_, ...), custom_call_target="tpu_custom_call" | custom-call | bytes 11796480 | tf_op jit(solution)/shard_map/pallas_call | solution.py:153
  218.2 7.1 %shard_map.133 = (bf16[288,2560]{1,0:T(8,128)(2,1)S(1)}, f32[1728,2560]{1,0:T(8,128)}, f32[1728,2560]{1,0:T(8,128)}) custom-call(s32[1]{0:T(128)} %bitcast.place, bf16[1728,768]{1,0:T(8,128)(2,1)S(1)} %maximum_bitcast_fusion.left, bf16[768,2560]{1,0:T(8,128)(2,1)S(1)} %copy-done.1, ...), custom_call_target="tpu_custom_call", output_to_operand_aliasing={{1}: (6, {}), {2}: (7, {})} | custom-call | flops 1132462080 | bytes 14745600 | tf_op jit(solution)/shard_map/pallas_call | solution.py:105
  225.3 2.0 collective-permute-start.12
  227.3 5.4 %shard_map.134 = (bf16[6912,2560]{1,0:T(8,128)(2,1)}, f32[8,128]{1,0:T(8,128)S(1)}) custom-call(s32[4]{0:T(128)S(1)} %pad_add_fusion.owners, bf16[288,2560]{1,0:T(8,128)(2,1)} %get-tuple-element.39.rest_0_, bf16[288,2560]{1,0:T(8,128)(2,1)} %collective-permute-done.9.rest_1_, ...), custom_call_target="tpu_custom_call", output_to_operand_aliasing={{0}: (5, {})} | custom-call | bytes 11796480 | tf_op jit(solution)/shard_map/pallas_call | solution.py:153
  232.6 7.1 %shard_map.135 = (bf16[288,2560]{1,0:T(8,128)(2,1)S(1)}, f32[1728,2560]{1,0:T(8,128)}, f32[1728,2560]{1,0:T(8,128)}) custom-call(s32[1]{0:T(128)} %bitcast.place, bf16[1728,768]{1,0:T(8,128)(2,1)S(1)} %maximum_bitcast_fusion.left, bf16[768,2560]{1,0:T(8,128)(2,1)S(1)} %copy-done.1, ...), custom_call_target="tpu_custom_call", output_to_operand_aliasing={{1}: (6, {}), {2}: (7, {})} | custom-call | flops 1132462080 | bytes 14745600 | tf_op jit(solution)/shard_map/pallas_call | solution.py:105
  240.2 19.5 %collective-permute-done.12.rest_1_ = bf16[288,2560]{1,0:T(8,128)(2,1)S(1)} collective-permute-done((bf16[288,2560]{1,0:T(8,128)(2,1)S(1)}, bf16[288,2560]{1,0:T(8,128)(2,1)S(1)}, u32[]{:S(2)}, u32[]{:S(2)}) %collective-permute-start.12) | collective-permute-done | bytes 1474592 | tf_op jit(solution)/shard_map/ppermute | solution.py:178
  260.9 30.5 %collective-permute-done.15.rest_1_ = bf16[288,2560]{1,0:T(8,128)(2,1)S(1)} collective-permute-done((bf16[288,2560]{1,0:T(8,128)(2,1)S(1)}, bf16[288,2560]{1,0:T(8,128)(2,1)S(1)}, u32[]{:S(2)}, u32[]{:S(2)}) %collective-permute-start.15) | collective-permute-done | bytes 1474592 | tf_op jit(solution)/shard_map/ppermute | solution.py:178
  292.1 4.4 %shard_map.136 = (bf16[6912,2560]{1,0:T(8,128)(2,1)}, f32[8,128]{1,0:T(8,128)S(1)}) custom-call(s32[4]{0:T(128)S(1)} %pad_add_fusion.owners, bf16[288,2560]{1,0:T(8,128)(2,1)S(1)} %get-tuple-element.44.rest_0_, bf16[288,2560]{1,0:T(8,128)(2,1)S(1)} %collective-permute-done.12.rest_1_, ...), custom_call_target="tpu_custom_call", output_to_operand_aliasing={{0}: (5, {})} | custom-call | bytes 11796480 | tf_op jit(solution)/shard_map/pallas_call | solution.py:153
  296.5 7.1 %shard_map.137 = (bf16[288,2560]{1,0:T(8,128)(2,1)S(1)}, f32[1728,2560]{1,0:T(8,128)}, f32[1728,2560]{1,0:T(8,128)}) custom-call(s32[1]{0:T(128)} %bitcast.place, bf16[1728,768]{1,0:T(8,128)(2,1)S(1)} %maximum_bitcast_fusion.left, bf16[768,2560]{1,0:T(8,128)(2,1)S(1)} %copy-done.1, ...), custom_call_target="tpu_custom_call", output_to_operand_aliasing={{1}: (6, {}), {2}: (7, {})} | custom-call | flops 1132462080 | bytes 14745600 | tf_op jit(solution)/shard_map/pallas_call | solution.py:105
  305.1 4.4 %shard_map.138 = (bf16[6912,2560]{1,0:T(8,128)(2,1)}, f32[8,128]{1,0:T(8,128)S(1)}) custom-call(s32[4]{0:T(128)S(1)} %pad_add_fusion.owners, bf16[288,2560]{1,0:T(8,128)(2,1)S(1)} %get-tuple-element.49.rest_0_, bf16[288,2560]{1,0:T(8,128)(2,1)S(1)} %collective-permute-done.15.rest_1_, ...), custom_call_target="tpu_custom_call", output_to_operand_aliasing={{0}: (5, {})} | custom-call | bytes 11796480 | tf_op jit(solution)/shard_map/pallas_call | solution.py:153
  309.5 7.1 %shard_map.139 = (bf16[288,2560]{1,0:T(8,128)(2,1)S(1)}, f32[1728,2560]{1,0:T(8,128)}, f32[1728,2560]{1,0:T(8,128)}) custom-call(s32[1]{0:T(128)} %bitcast.place, bf16[1728,768]{1,0:T(8,128)(2,1)S(1)} %maximum_bitcast_fusion.left, bf16[768,2560]{1,0:T(8,128)(2,1)S(1)} %copy-done.1, ...), custom_call_target="tpu_custom_call", output_to_operand_aliasing={{1}: (6, {}), {2}: (7, {})} | custom-call | flops 1132462080 | bytes 14745600 | tf_op jit(solution)/shard_map/pallas_call | solution.py:105
  317.1 20.4 %collective-permute-done.21.rest_1_ = bf16[288,2560]{1,0:T(8,128)(2,1)S(1)} collective-permute-done((bf16[288,2560]{1,0:T(8,128)(2,1)S(1)}, bf16[288,2560]{1,0:T(8,128)(2,1)S(1)}, u32[]{:S(2)}, u32[]{:S(2)}) %collective-permute-start.21) | collective-permute-done | bytes 1474592 | tf_op jit(solution)/shard_map/ppermute | solution.py:178
  338.7 30.4 %collective-permute-done.18.rest_1_ = bf16[288,2560]{1,0:T(8,128)(2,1)S(1)} collective-permute-done((bf16[288,2560]{1,0:T(8,128)(2,1)S(1)}, bf16[288,2560]{1,0:T(8,128)(2,1)S(1)}, u32[]{:S(2)}, u32[]{:S(2)}) %collective-permute-start.18) | collective-permute-done | bytes 1474592 | tf_op jit(solution)/shard_map/ppermute | solution.py:178
  369.9 5.0 %shard_map.140 = (bf16[6912,2560]{1,0:T(8,128)(2,1)}, f32[8,128]{1,0:T(8,128)}) custom-call(s32[4]{0:T(128)S(1)} %pad_add_fusion.owners, bf16[288,2560]{1,0:T(8,128)(2,1)S(1)} %get-tuple-element.53.rest_0_, bf16[288,2560]{1,0:T(8,128)(2,1)S(1)} %collective-permute-done.21.rest_1_, ...), custom_call_target="tpu_custom_call", output_to_operand_aliasing={{0}: (5, {})} | custom-call | bytes 11796480 | tf_op jit(solution)/shard_map/pallas_call | solution.py:153
  374.9 5.0 %shard_map.141 = (bf16[6912,2560]{1,0:T(8,128)(2,1)}, f32[8,128]{1,0:T(8,128)}) custom-call(s32[4]{0:T(128)S(1)} %pad_add_fusion.owners, bf16[288,2560]{1,0:T(8,128)(2,1)S(1)} %get-tuple-element.52.rest_0_, bf16[288,2560]{1,0:T(8,128)(2,1)S(1)} %collective-permute-done.18.rest_1_, ...), custom_call_target="tpu_custom_call", output_to_operand_aliasing={{0}: (5, {})} | custom-call | bytes 11796480 | tf_op jit(solution)/shard_map/pallas_call | solution.py:153
  (76 shorter events, 20.6 us)
Async XLA Ops:
  7.2 43.9 %all-gather.2.cloned.1.call-start = ((), (), s32[]{:S(2)}) async-start(), calls=%async_computation | async-start | bytes 3981312 | tf_op jit(solution)/shard_map/all_gather | solution.py:205
  7.9 116.2 %collective-permute-start.3 = (bf16[192,2560]{1,0:T(8,128)(2,1)}, bf16[192,2560]{1,0:T(8,128)(2,1)}, u32[]{:S(2)}, u32[]{:S(2)}) collective-permute-start(bf16[192,2560]{1,0:T(8,128)(2,1)} %param.13), channel_id=1, source_target_pairs={{0,4},{4,8},{8,12},{12,0},{1,5},{5,9},{9,13},{13,1},{2,6},{6,10},{... | collective-permute-start | bytes 2949128 | tf_op jit(solution)/shard_map/ppermute | solution.py:217
  10.6 115.2 %collective-permute-start.4 = (bf16[192,2560]{1,0:T(8,128)(2,1)}, bf16[192,2560]{1,0:T(8,128)(2,1)}, u32[]{:S(2)}, u32[]{:S(2)}) collective-permute-start(bf16[192,2560]{1,0:T(8,128)(2,1)} %param.13), channel_id=1, source_target_pairs={{0,8},{4,12},{8,0},{12,4},{1,9},{5,13},{9,1},{13,5},{2,10},{6,14},... | collective-permute-start | bytes 2949128 | tf_op jit(solution)/shard_map/ppermute | solution.py:217
  10.6 115.2 %collective-permute-start.5 = (bf16[192,2560]{1,0:T(8,128)(2,1)}, bf16[192,2560]{1,0:T(8,128)(2,1)}, u32[]{:S(2)}, u32[]{:S(2)}) collective-permute-start(bf16[192,2560]{1,0:T(8,128)(2,1)} %param.13), channel_id=1, source_target_pairs={{0,12},{4,0},{8,4},{12,8},{1,13},{5,1},{9,5},{13,9},{2,14},{6,2},{... | collective-permute-start | bytes 2949128 | tf_op jit(solution)/shard_map/ppermute | solution.py:217
  63.6 4.8 %copy-start.2 = (bf16[192,1,1728]{2,1,0:T(2,128)(2,1)S(1)}, bf16[192,1,1728]{2,1,0:T(2,128)(2,1)}, u32[]{:S(2)}) copy-start(bf16[192,1,1728]{2,1,0:T(2,128)(2,1)} %get-tuple-element.63) | copy-start | bytes 1990660
  64.5 64.9 %collective-permute-start = (bf16[192,1728]{1,0:T(8,128)(2,1)}, bf16[192,1728]{1,0:T(8,128)(2,1)}, u32[]{:S(2)}, u32[]{:S(2)}) collective-permute-start(bf16[192,1728]{1,0:T(8,128)(2,1)} %bitcast.42), channel_id=1, source_target_pairs={{0,4},{4,8},{8,12},{12,0},{1,5},{5,9},{9,13},{13,1},{2,6},{6,10},{... | collective-permute-start | bytes 1990664 | tf_op jit(solution)/shard_map/ppermute | solution.py:216
  66.3 3.8 copy-start.3
  67.2 64.6 %collective-permute-start.1 = (bf16[192,1728]{1,0:T(8,128)(2,1)}, bf16[192,1728]{1,0:T(8,128)(2,1)}, u32[]{:S(2)}, u32[]{:S(2)}) collective-permute-start(bf16[192,1728]{1,0:T(8,128)(2,1)} %bitcast.41), channel_id=1, source_target_pairs={{0,8},{4,12},{8,0},{12,4},{1,9},{5,13},{9,1},{13,5},{2,10},{6,14},... | collective-permute-start | bytes 1990664 | tf_op jit(solution)/shard_map/ppermute | solution.py:216
  70.1 15.6 %copy-start.5 = (f32[192]{0:T(256)S(1)}, f32[192]{0:T(256)}, u32[]{:S(2)}) copy-start(f32[192]{0:T(256)} %param.14) | copy-start | bytes 2308
  70.2 15.7 %copy-start.6 = (f32[4]{0:T(128)S(1)}, f32[4]{0:T(128)}, u32[]{:S(2)}) copy-start(f32[4]{0:T(128)} %compare_convert_fusion.1) | copy-start | bytes 52
  70.2 53.9 %copy-start.4 = (bf16[192,1,1728]{2,0,1:T(8,128)(2,1)S(1)}, bf16[192,1,1728]{2,0,1:T(8,128)(2,1)}, u32[]{:S(2)}) copy-start(bf16[192,1,1728]{2,0,1:T(8,128)(2,1)} %copy.54) | copy-start | bytes 1990660
  124.1 12.2 %collective-permute-start.2 = (bf16[192,1728]{1,0:T(8,128)(2,1)S(1)}, bf16[192,1728]{1,0:T(8,128)(2,1)S(1)}, u32[]{:S(2)}, u32[]{:S(2)}) collective-permute-start(bf16[192,1728]{1,0:T(8,128)(2,1)S(1)} %bitcast.58), channel_id=1, source_target_pairs={{0,12},{4,0},{8,4},{12,8},{1,13},{5,1},{9,5},{13,9},{2,14},{6,2},{... | collective-permute-start | bytes 1990664 | tf_op jit(solution)/shard_map/ppermute | solution.py:216
  137.5 3.1 copy-start
  147.8 34.7 %collective-permute-start.6 = (bf16[288,2560]{1,0:T(8,128)(2,1)}, bf16[288,2560]{1,0:T(8,128)(2,1)}, u32[]{:S(2)}, u32[]{:S(2)}) collective-permute-start(bf16[288,2560]{1,0:T(8,128)(2,1)} %get-tuple-element.35.rest_0_), channel_id=1, source_target_pairs={{0,8},{4,12},{8,0},{12,4},{1,9},{5,13},{9,1},{13,5},{2,10},{6,14},... | collective-permute-start | bytes 4423688 | tf_op jit(solution)/shard_map/ppermute | solution.py:178
  155.0 57.4 %collective-permute-start.9 = (bf16[288,2560]{1,0:T(8,128)(2,1)}, bf16[288,2560]{1,0:T(8,128)(2,1)}, u32[]{:S(2)}, u32[]{:S(2)}) collective-permute-start(bf16[288,2560]{1,0:T(8,128)(2,1)} %get-tuple-element.39.rest_0_), channel_id=1, source_target_pairs={{0,8},{4,12},{8,0},{12,4},{1,9},{5,13},{9,1},{13,5},{2,10},{6,14},... | collective-permute-start | bytes 4423688 | tf_op jit(solution)/shard_map/ppermute | solution.py:178
  156.5 56.0 %collective-permute-start.7 = (bf16[288,2560]{1,0:T(8,128)(2,1)}, bf16[288,2560]{1,0:T(8,128)(2,1)}, u32[]{:S(2)}, u32[]{:S(2)}) collective-permute-start(bf16[288,2560]{1,0:T(8,128)(2,1)} %get-tuple-element.35.rest_0_), channel_id=1, source_target_pairs={{0,4},{4,0},{8,12},{12,8},{1,5},{5,1},{9,13},{13,9},{2,6},{6,2},{1... | collective-permute-start | bytes 4423688 | tf_op jit(solution)/shard_map/ppermute | solution.py:183
  182.5 30.0 %collective-permute-start.8 = (bf16[288,2560]{1,0:T(8,128)(2,1)}, bf16[288,2560]{1,0:T(8,128)(2,1)}, u32[]{:S(2)}, u32[]{:S(2)}) collective-permute-start(bf16[288,2560]{1,0:T(8,128)(2,1)} %collective-permute-done.6.rest_1_), channel_id=1, source_target_pairs={{0,4},{4,0},{8,12},{12,8},{1,5},{5,1},{9,13},{13,9},{2,6},{6,2},{1... | collective-permute-start | bytes 4423688 | tf_op jit(solution)/shard_map/ppermute | solution.py:183
  182.5 44.8 %collective-permute-start.10 = (bf16[288,2560]{1,0:T(8,128)(2,1)}, bf16[288,2560]{1,0:T(8,128)(2,1)}, u32[]{:S(2)}, u32[]{:S(2)}) collective-permute-start(bf16[288,2560]{1,0:T(8,128)(2,1)} %get-tuple-element.39.rest_0_), channel_id=1, source_target_pairs={{0,4},{4,0},{8,12},{12,8},{1,5},{5,1},{9,13},{13,9},{2,6},{6,2},{1... | collective-permute-start | bytes 4423688 | tf_op jit(solution)/shard_map/ppermute | solution.py:183
  212.4 14.8 %collective-permute-start.11 = (bf16[288,2560]{1,0:T(8,128)(2,1)}, bf16[288,2560]{1,0:T(8,128)(2,1)}, u32[]{:S(2)}, u32[]{:S(2)}) collective-permute-start(bf16[288,2560]{1,0:T(8,128)(2,1)} %collective-permute-done.9.rest_1_), channel_id=1, source_target_pairs={{0,4},{4,0},{8,12},{12,8},{1,5},{5,1},{9,13},{13,9},{2,6},{6,2},{1... | collective-permute-start | bytes 4423688 | tf_op jit(solution)/shard_map/ppermute | solution.py:183
  212.5 5.7 %copy-start.1 = (bf16[768,2560]{1,0:T(8,128)(2,1)S(1)}, bf16[768,2560]{1,0:T(8,128)(2,1)}, u32[]{:S(2)}) copy-start(bf16[768,2560]{1,0:T(8,128)(2,1)} %multiply_convert_fusion.right) | copy-start | bytes 11796484
  225.3 34.5 %collective-permute-start.12 = (bf16[288,2560]{1,0:T(8,128)(2,1)S(1)}, bf16[288,2560]{1,0:T(8,128)(2,1)S(1)}, u32[]{:S(2)}, u32[]{:S(2)}) collective-permute-start(bf16[288,2560]{1,0:T(8,128)(2,1)S(1)} %get-tuple-element.44.rest_0_), channel_id=1, source_target_pairs={{0,8},{4,12},{8,0},{12,4},{1,9},{5,13},{9,1},{13,5},{2,10},{6,14},... | collective-permute-start | bytes 4423688 | tf_op jit(solution)/shard_map/ppermute | solution.py:178
  239.7 51.6 %collective-permute-start.15 = (bf16[288,2560]{1,0:T(8,128)(2,1)S(1)}, bf16[288,2560]{1,0:T(8,128)(2,1)S(1)}, u32[]{:S(2)}, u32[]{:S(2)}) collective-permute-start(bf16[288,2560]{1,0:T(8,128)(2,1)S(1)} %get-tuple-element.49.rest_0_), channel_id=1, source_target_pairs={{0,8},{4,12},{8,0},{12,4},{1,9},{5,13},{9,1},{13,5},{2,10},{6,14},... | collective-permute-start | bytes 4423688 | tf_op jit(solution)/shard_map/ppermute | solution.py:178
  239.7 52.4 %collective-permute-start.13 = (bf16[288,2560]{1,0:T(8,128)(2,1)S(1)}, bf16[288,2560]{1,0:T(8,128)(2,1)S(1)}, u32[]{:S(2)}, u32[]{:S(2)}) collective-permute-start(bf16[288,2560]{1,0:T(8,128)(2,1)S(1)} %get-tuple-element.44.rest_0_), channel_id=1, source_target_pairs={{0,4},{4,0},{8,12},{12,8},{1,5},{5,1},{9,13},{13,9},{2,6},{6,2},{1... | collective-permute-start | bytes 4423688 | tf_op jit(solution)/shard_map/ppermute | solution.py:183
  259.8 32.3 %collective-permute-start.14 = (bf16[288,2560]{1,0:T(8,128)(2,1)S(1)}, bf16[288,2560]{1,0:T(8,128)(2,1)S(1)}, u32[]{:S(2)}, u32[]{:S(2)}) collective-permute-start(bf16[288,2560]{1,0:T(8,128)(2,1)S(1)} %collective-permute-done.12.rest_1_), channel_id=1, source_target_pairs={{0,4},{4,0},{8,12},{12,8},{1,5},{5,1},{9,13},{13,9},{2,6},{6,2},{1... | collective-permute-start | bytes 4423688 | tf_op jit(solution)/shard_map/ppermute | solution.py:183
  260.8 44.2 %collective-permute-start.16 = (bf16[288,2560]{1,0:T(8,128)(2,1)S(1)}, bf16[288,2560]{1,0:T(8,128)(2,1)S(1)}, u32[]{:S(2)}, u32[]{:S(2)}) collective-permute-start(bf16[288,2560]{1,0:T(8,128)(2,1)S(1)} %get-tuple-element.49.rest_0_), channel_id=1, source_target_pairs={{0,4},{4,0},{8,12},{12,8},{1,5},{5,1},{9,13},{13,9},{2,6},{6,2},{1... | collective-permute-start | bytes 4423688 | tf_op jit(solution)/shard_map/ppermute | solution.py:183
  291.4 13.7 %collective-permute-start.17 = (bf16[288,2560]{1,0:T(8,128)(2,1)S(1)}, bf16[288,2560]{1,0:T(8,128)(2,1)S(1)}, u32[]{:S(2)}, u32[]{:S(2)}) collective-permute-start(bf16[288,2560]{1,0:T(8,128)(2,1)S(1)} %collective-permute-done.15.rest_1_), channel_id=1, source_target_pairs={{0,4},{4,0},{8,12},{12,8},{1,5},{5,1},{9,13},{13,9},{2,6},{6,2},{1... | collective-permute-start | bytes 4423688 | tf_op jit(solution)/shard_map/ppermute | solution.py:183
  303.6 33.9 %collective-permute-start.21 = (bf16[288,2560]{1,0:T(8,128)(2,1)S(1)}, bf16[288,2560]{1,0:T(8,128)(2,1)S(1)}, u32[]{:S(2)}, u32[]{:S(2)}) collective-permute-start(bf16[288,2560]{1,0:T(8,128)(2,1)S(1)} %get-tuple-element.53.rest_0_), channel_id=1, source_target_pairs={{0,8},{4,12},{8,0},{12,4},{1,9},{5,13},{9,1},{13,5},{2,10},{6,14},... | collective-permute-start | bytes 4423688 | tf_op jit(solution)/shard_map/ppermute | solution.py:178
  316.5 52.6 %collective-permute-start.18 = (bf16[288,2560]{1,0:T(8,128)(2,1)S(1)}, bf16[288,2560]{1,0:T(8,128)(2,1)S(1)}, u32[]{:S(2)}, u32[]{:S(2)}) collective-permute-start(bf16[288,2560]{1,0:T(8,128)(2,1)S(1)} %get-tuple-element.52.rest_0_), channel_id=1, source_target_pairs={{0,8},{4,12},{8,0},{12,4},{1,9},{5,13},{9,1},{13,5},{2,10},{6,14},... | collective-permute-start | bytes 4423688 | tf_op jit(solution)/shard_map/ppermute | solution.py:178
  316.5 53.4 %collective-permute-start.22 = (bf16[288,2560]{1,0:T(8,128)(2,1)S(1)}, bf16[288,2560]{1,0:T(8,128)(2,1)S(1)}, u32[]{:S(2)}, u32[]{:S(2)}) collective-permute-start(bf16[288,2560]{1,0:T(8,128)(2,1)S(1)} %get-tuple-element.53.rest_0_), channel_id=1, source_target_pairs={{0,4},{4,0},{8,12},{12,8},{1,5},{5,1},{9,13},{13,9},{2,6},{6,2},{1... | collective-permute-start | bytes 4423688 | tf_op jit(solution)/shard_map/ppermute | solution.py:183
  337.5 32.4 %collective-permute-start.23 = (bf16[288,2560]{1,0:T(8,128)(2,1)S(1)}, bf16[288,2560]{1,0:T(8,128)(2,1)S(1)}, u32[]{:S(2)}, u32[]{:S(2)}) collective-permute-start(bf16[288,2560]{1,0:T(8,128)(2,1)S(1)} %collective-permute-done.21.rest_1_), channel_id=1, source_target_pairs={{0,4},{4,0},{8,12},{12,8},{1,5},{5,1},{9,13},{13,9},{2,6},{6,2},{1... | collective-permute-start | bytes 4423688 | tf_op jit(solution)/shard_map/ppermute | solution.py:183
  338.7 36.2 %collective-permute-start.19 = (bf16[288,2560]{1,0:T(8,128)(2,1)S(1)}, bf16[288,2560]{1,0:T(8,128)(2,1)S(1)}, u32[]{:S(2)}, u32[]{:S(2)}) collective-permute-start(bf16[288,2560]{1,0:T(8,128)(2,1)S(1)} %get-tuple-element.52.rest_0_), channel_id=1, source_target_pairs={{0,4},{4,0},{8,12},{12,8},{1,5},{5,1},{9,13},{13,9},{2,6},{6,2},{1... | collective-permute-start | bytes 4423688 | tf_op jit(solution)/shard_map/ppermute | solution.py:183
  369.1 5.8 %collective-permute-start.20 = (bf16[288,2560]{1,0:T(8,128)(2,1)S(1)}, bf16[288,2560]{1,0:T(8,128)(2,1)S(1)}, u32[]{:S(2)}, u32[]{:S(2)}) collective-permute-start(bf16[288,2560]{1,0:T(8,128)(2,1)S(1)} %collective-permute-done.18.rest_1_), channel_id=1, source_target_pairs={{0,4},{4,0},{8,12},{12,8},{1,5},{5,1},{9,13},{13,9},{2,6},{6,2},{1... | collective-permute-start | bytes 4423688 | tf_op jit(solution)/shard_map/ppermute | solution.py:183
Sparse Core Ops, SparseCore 0:
  9.5 41.4 all-gather.1

commit v3 on v2

--- a/solution.py
+++ b/solution.py
@@ -70,40 +70,43 @@
     return ((current - learn_rate * update).astype(jnp.bfloat16), new_first, new_second)
 
 
-def update_kernel(place, left, right, weight, first, second, *rest):
-    updated, new_first, new_second = rest[-3:]
-    gradient = jnp.dot(left[...], right[...], preferred_element_type=jnp.float32)
+def update_kernel(count, place, *refs):
+    weight, first, second = refs[2 * count : 2 * count + 3]
+    updated, new_first, new_second = refs[-3:]
+    gradient = jnp.dot(refs[0][...], refs[count][...], preferred_element_type=jnp.float32)
+    for i in range(1, count):
+        gradient += jnp.dot(
+            refs[i][...], refs[count + i][...], preferred_element_type=jnp.float32
+        )
     updated[...], new_first[...], new_second[...] = adam_rows(
         weight[...], first[...], second[...], gradient
     )
 
 
-def update_rows(place, left, right, weight, first, second, carried, after, start, rows, tile):
+def update_rows(place, left, right, weight, first, second, carried, start, rows, tile):
     columns = weight.shape[1]
-    tokens = right.shape[0]
+    count = len(left)
+    tokens = right[0].shape[0]
     tiles = rows // tile
     begin = start // tile
     shard_tiles = first.shape[0] // tile
     here = lambda i, place: (begin + i, 0)
     moment = pl.BlockSpec((tile, columns), here)
     in_specs = [
-        pl.BlockSpec((tile, tokens), here),
-        pl.BlockSpec((tokens, columns), lambda i, place: (0, 0)),
+        *[pl.BlockSpec((tile, tokens), here)] * count,
+        *[pl.BlockSpec((tokens, columns), lambda i, place: (0, 0))] * count,
         pl.BlockSpec((tile, columns), lambda i, place: (place[0] * shard_tiles + begin + i, 0)),
         moment,
         moment,
     ]
-    operands = [left, right, weight, first, second]
+    operands = [*left, *right, weight, first, second]
     aliases = {}
     if carried is not None:
         in_specs += [pl.BlockSpec(memory_space=pl.ANY)] * 2
         operands += list(carried)
-        aliases = {6: 1, 7: 2}
-    if after is not None:
-        in_specs.append(pl.BlockSpec(memory_space=pl.ANY))
-        operands.append(after)
+        aliases = {2 * count + 4: 1, 2 * count + 5: 2}
     return pl.pallas_call(
-        update_kernel,
+        functools.partial(update_kernel, count),
         grid_spec=pltpu.PrefetchScalarGridSpec(
             num_scalar_prefetch=1,
             grid=(tiles,),
@@ -118,7 +121,7 @@
         input_output_aliases=aliases,
         compiler_params=pltpu.CompilerParams(vmem_limit_bytes=40 * 2**20),
         cost_estimate=pl.CostEstimate(
-            flops=2 * rows * tokens * columns,
+            flops=2 * rows * count * tokens * columns,
             bytes_accessed=20 * rows * columns,
             transcendentals=rows * columns,
         ),
@@ -171,17 +174,35 @@
     )(owners, *operands)
 
 
-def spread(chunk, me, count):
-    pieces = [(me, chunk)]
+def gate_kernel(*refs):
+    pass
+
+
+def gate(piece, *tokens):
+    anywhere = pl.BlockSpec(memory_space=pl.ANY)
+    return pl.pallas_call(
+        gate_kernel,
+        in_specs=[anywhere] * (1 + len(tokens)),
+        out_specs=anywhere,
+        out_shape=jax.ShapeDtypeStruct(piece.shape, piece.dtype),
+        input_output_aliases={0: 0},
+    )(piece, *tokens)
+
+
+def send_far(chunk, me, count):
     stride = 2 if count % 2 == 0 else 1
+    far = []
     for hop in range(stride, count, stride):
         sent = lax.ppermute(chunk, "dp", [(i, (i + hop) % count) for i in range(count)])
-        pieces.append((lax.rem(me - hop + count, count), sent))
-    if stride == 2:
-        swap = [(i, i ^ 1) for i in range(count)]
-        for owner, piece in list(pieces):
-            pieces.append((owner ^ 1, lax.ppermute(piece, "dp", swap)))
-    return pieces
+        far.append((lax.rem(me - hop + count, count), sent))
+    return far
+
+
+def send_near(pieces, count):
+    if count % 2:
+        return pieces
+    swap = [(i, i ^ 1) for i in range(count)]
+    return pieces + [(owner ^ 1, lax.ppermute(piece, "dp", swap)) for owner, piece in pieces]
 
 
 def on_device(
@@ -202,60 +223,49 @@
     shard_rows = first_moment.shape[1]
     shifts = [[(i, (i + hop) % count) for i in range(count)] for hop in range(1, count)]
 
-    gathered = lax.all_gather(activations, "section", axis=0, tiled=True)
+    sections = lax.axis_size("section")
+    section = lax.axis_index("section")
+    halves = [activations]
+    for hop in range(1, sections):
+        shift = [(i, (i + hop) % sections) for i in range(sections)]
+        halves.append(lax.ppermute(activations, "section", shift))
+    gathered = jnp.concatenate(
+        [
+            lax.select_n(lax.rem(section - j + sections, sections), *halves)
+            for j in range(sections)
+        ]
+    )
     tok_rep = gathered.shape[0]
-    tokens = count * tok_rep
-    blocks = gathered.reshape(tok_rep, count, shard_rows)
+    turned = gathered.T
 
     def block_for(owner):
-        return lax.dynamic_index_in_dim(blocks, owner, axis=1, keepdims=False)
+        return lax.dynamic_slice_in_dim(turned, owner * shard_rows, shard_rows, 0)
 
     left = [block_for(me)]
     right = [readout]
     for hop in range(1, count):
         left.append(lax.ppermute(block_for(lax.rem(me + hop, count)), "dp", shifts[hop - 1]))
         right.append(lax.ppermute(readout, "dp", shifts[hop - 1]))
-    order = [lax.rem(me - hop + count, count) for hop in range(count)]
 
     layer_out = jnp.dot(gathered, weight, preferred_element_type=jnp.float32)
     score_share = jnp.sum(layer_out * readout.astype(jnp.float32), axis=1)
-    first_holder = (lax.axis_index("section") + lax.axis_index("mp")) == 0
-    once = jnp.where(first_holder, 1.0, 0.0).astype(jnp.float32)
-    mine = jnp.stack([score_share + once * logp_rest, once * old_logp, once * ref_logp])
-    slots = (jnp.arange(count) == me).astype(jnp.float32)
-    known = lax.psum(mine[:, None, :] * slots[None, :, None], ("section", "dp", "mp"))
-    known = known.reshape(3, tokens)
-    positions = jnp.arange(tokens, dtype=jnp.int32)
+    score_share = gate(score_share[None], *left)[0]
+    new_logp = logp_rest + lax.psum(score_share, ("section", "mp"))
+    positions = me * tok_rep + jnp.arange(tok_rep, dtype=jnp.int32)
     adv_token, token_weight = token_terms(lengths, group_ids, rewards, positions, RESP_LEN)
-    coeff = token_coeff(known[0], known[1], known[2], adv_token, token_weight)
-    coeff = coeff.reshape(count, tok_rep)
-    coeff = jnp.concatenate(
-        [lax.dynamic_index_in_dim(coeff, owner, axis=0, keepdims=False) for owner in order]
-    )
-
-    left = jnp.concatenate(left, axis=0).T
-    right = jnp.concatenate(right, axis=0)
-    weighted = (coeff[:, None] * right.astype(jnp.float32)).astype(jnp.bfloat16)
+    coeff = token_coeff(new_logp, old_logp, ref_logp, adv_token, token_weight)
+    coeffs = [coeff] + [lax.ppermute(coeff, "dp", shift) for shift in shifts]
+    weighted = []
+    for here, block in zip(coeffs, right):
+        weighted.append((here[:, None] * block.astype(jnp.float32)).astype(jnp.bfloat16))
 
     chunks = max(n for n in range(1, 7) if shard_rows % (16 * n) == 0)
     rows = shard_rows // chunks
     tile = rows // 2 if rows % 32 == 0 else rows
     where_am_i = me.reshape(1).astype(jnp.int32)
     moments = new_weight = None
-    sent, placed = [], []
-
-    def place(chunk):
-        pieces = sent[chunk]
-        owners = jnp.stack([owner for owner, _ in pieces]).astype(jnp.int32)
-        whole, token = place_rows(
-            owners, [piece for _, piece in pieces], new_weight, shard_rows, chunk * rows
-        )
-        placed.append(token)
-        return whole
-
+    sent, tokens = [], []
     for chunk in range(chunks):
-        if chunk >= 2:
-            new_weight = place(chunk - 2)
         updated, *moments = update_rows(
             where_am_i,
             left,
@@ -264,14 +274,22 @@
             first_moment[0],
             second_moment[0],
             moments,
-            placed[-1] if placed else None,
             chunk * rows,
             rows,
             tile,
         )
-        sent.append(spread(updated, me, count))
-    for chunk in range(max(chunks - 2, 0), chunks):
-        new_weight = place(chunk)
+        sent.append((updated, send_far(updated, me, count)))
+    for chunk, (own, far) in enumerate(sent):
+        if chunk == 1:
+            far = [(owner, gate(piece, sent[-1][0])) for owner, piece in far]
+        if chunk == chunks - 1 and chunk > 2:
+            far = [(owner, gate(piece, tokens[chunk - 2])) for owner, piece in far]
+        pieces = send_near([(me, own)] + far, count)
+        owners = jnp.stack([owner for owner, _ in pieces]).astype(jnp.int32)
+        new_weight, token = place_rows(
+            owners, [piece for _, piece in pieces], new_weight, shard_rows, chunk * rows
+        )
+        tokens.append(token)
     return (new_weight, moments[0][None], moments[1][None])
 
 

time: 387 us -> 325 us (0.84)
  waiting for transfers between devices: 195 us -> 150 us
  blocking collectives: 38 us -> 18.7 us
  between operations: 14.3 us -> 1.11 us
  Pallas kernels: 72.3 us -> 81.3 us
  starting transfers between devices: 17.3 us -> 23.1 us
    all_gather x1 -> x0, waiting for transfers between devices: 35.3 us -> none  [on_device(): gathered = lax.all_gather(activations, 'section', axis=0, tiled=True)]
    psum x1, blocking collectives: 38 us -> 18.7 us  [on_device(): new_logp = logp_rest + lax.psum(score_share, ('section', 'mp'))]
    ppermute x18 -> x22, waiting for transfers between devices: 156 us -> 143 us  [the longest x6 119 us: send_far(): lax.ppermute(chunk, 'dp', [(i, (i + hop) % count) for i in range(count)])]
    ppermute x18 -> x22, starting transfers between devices: 10.4 us -> 16.7 us  [the longest x12 6.69 us: send_near(): lax.ppermute(piece, 'dp', swap)]
    reshape x1 -> x0, local copies, waits for them, and re-layouts: 6.06 us -> none  [on_device(): blocks = gathered.reshape(tok_rep, count, shard_rows)]
    ppermute x3, waiting for transfers between devices: 2.21 us -> 7.72 us  [on_device(): lax.ppermute(block_for(lax.rem(me + hop, count)), 'dp', shifts[hop - 1])]
    pallas_call x6 -> x9, Pallas kernels: 42.7 us -> 47.6 us  [the longest x6 47.6 us: update_rows(): pl.pallas_call(functools.partial(update_kernel, count), grid_spec=pltpu.P...]
    pallas_call x6, Pallas kernels: 29.7 us -> 33.7 us  [place_rows(): pl.pallas_call(functools.partial(place_kernel, count, shard_rows, start),...]
  transfers between devices with their start and end apart: 25 -> 28, of which waited for: 8 -> 8; matrix products, arithmetic and copies ran while one was open for 12% -> 14% of each run, Pallas kernels for 16% -> 21%
where the time goes in v3:
time: 325 us
  waiting for transfers between devices  150 us (46%)
  Pallas kernels  81.3 us (25%)
  local copies, waits for them, and re-layouts  23.8 us (7%)
  starting transfers between devices  23.1 us (7%)
  blocking collectives  18.7 us (6%)
  matrix products  15.1 us (5%)
  other arithmetic  11 us (3%)
    ppermute x6, waiting for transfers between devices, send_far(): lax.ppermute(chunk, 'dp', [(i, (i + hop) % count) for i in range(count)])  119 us
    pallas_call x6, Pallas kernels, update_rows(): pl.pallas_call(functools.partial(update_kernel, count), grid_spec=pltpu.P...  47.6 us
    pallas_call x6, Pallas kernels, place_rows(): pl.pallas_call(functools.partial(place_kernel, count, shard_rows, start),...  33.7 us
    ppermute x1, waiting for transfers between devices, on_device(): halves.append(lax.ppermute(activations, 'section', shift))  23.8 us
    psum x1, blocking collectives, on_device(): new_logp = logp_rest + lax.psum(score_share, ('section', 'mp'))  18.7 us
    dot_general x1, matrix products, on_device(): layer_out = jnp.dot(gathered, weight, preferred_element_type=jnp.float32)  15.1 us
    unnamed x39, local copies, waits for them, and re-layouts  8.24 us
    ppermute x3, waiting for transfers between devices, on_device(): lax.ppermute(block_for(lax.rem(me + hop, count)), 'dp', shifts[hop - 1])  7.72 us
  transfers between devices with their start and end apart: 28, of which 8 were waited for; matrix products, arithmetic and copies ran while one was open for 14% of the time, Pallas kernels for 21%

profile of v3, /device:TPU:1, one launch (start us, length us, event | category | flops | bytes accessed | tf_op | source)
XLA Modules:
  0.0 324.5 jit_solution(17488477693827940278)
XLA Ops:
  5.0 2.6 copy.63
  8.1 23.8 %collective-permute-done = bf16[96,6912]{1,0:T(8,128)(2,1)S(1)} collective-permute-done((bf16[96,6912]{1,0:T(8,128)(2,1)}, bf16[96,6912]{1,0:T(8,128)(2,1)S(1)}, u32[]{:S(2)}, u32[]{:S(2)}) %collective-permute-start) | collective-permute-done | bytes 1327136 | tf_op jit(solution)/shard_map/ppermute | solution.py:231
  35.9 3.4 %fusion.9 = (bf16[1728,192]{1,0:T(8,128)(2,1)}, bf16[1728,192]{1,0:T(8,128)(2,1)}, bf16[1728,192]{1,0:T(8,128)(2,1)}, bf16[1728,192]{1,0:T(8,128)(2,1)}) fusion(s32[]{:T(128)S(6)} %select_n.87, bf16[96,6912]{0,1:T(8,128)(2,1)S(1)} %get-tuple-element.62, bf16[96,6912]{0,1:T(8,128)(2,1)S(1)} %get-tuple-element.61, s32[]{:T(128)S(6)} %select_n.84, ...), kind=kLoop, calls=%fused_computation.25 | loop fusion | flops 5308416 | bytes 5308432 | tf_op jit(solution)/shard_map/dynamic_slice | solution.py:242
  39.3 2.3 copy.67
  41.6 2.4 collective-permute-start.1
  44.1 2.3 copy.68
  46.4 2.3 copy.69
  49.1 15.1 %fusion.1 = f32[192]{0:T(256)} fusion(bf16[192,2560]{1,0:T(8,128)(2,1)} %param.13, bf16[6912,2560]{1,0:T(8,128)(2,1)} %refs_8_.11, bf16[96,6912]{0,1:T(8,128)(2,1)S(1)} %get-tuple-element.61, bf16[96,6912]{0,1:T(8,128)(2,1)S(1)} %get-tuple-element.62), kind=kOutput, calls=%fused_computation.17 | convolution fusion | flops 6801555456 | bytes 39027456 | tf_op jit(solution)/shard_map/dot_general | solution.py:250
  65.6 2.3 copy.88.refs_2_.refs_1_
  68.0 3.9 %collective-permute-done.2 = bf16[1728,192]{0,1:T(8,128)(2,1)} collective-permute-done((bf16[1728,192]{0,1:T(8,128)(2,1)}, bf16[1728,192]{0,1:T(8,128)(2,1)}, u32[]{:S(2)}, u32[]{:S(2)}) %collective-permute-start.2) | collective-permute-done | bytes 663584 | tf_op jit(solution)/shard_map/ppermute | solution.py:247
  71.9 2.3 copy.89.refs_3_.refs_2_
  74.2 3.8 %collective-permute-done.3 = bf16[1728,192]{0,1:T(8,128)(2,1)} collective-permute-done((bf16[1728,192]{0,1:T(8,128)(2,1)}, bf16[1728,192]{0,1:T(8,128)(2,1)}, u32[]{:S(2)}, u32[]{:S(2)}) %collective-permute-start.3) | collective-permute-done | bytes 663584 | tf_op jit(solution)/shard_map/ppermute | solution.py:247
  78.0 2.4 copy.90.refs_4_.refs_3_
  80.3 18.7 %psum.7 = f32[192]{0:T(256)S(1)} all-reduce(f32[192]{0:T(256)} %bitcast.34), channel_id=1, replica_groups=mesh['section'=2,'dp'=4,'mp'=4] {'section','mp'}, use_global_device_ids=true, to_apply=%region_2.0 | all-reduce | flops 192 | bytes 1536 | tf_op jit(solution)/shard_map/psum | solution.py:253
  99.1 3.1 collective-permute-start.8
  109.1 8.0 %shard_map.131 = (bf16[288,2560]{1,0:T(8,128)(2,1)}, f32[1728,2560]{1,0:T(8,128)}, f32[1728,2560]{1,0:T(8,128)}) custom-call(s32[1]{0:T(128)} %bitcast.place, bf16[1728,192]{1,0:T(8,128)(2,1)S(1)} %copy-done.3, bf16[1728,192]{1,0:T(8,128)(2,1)S(1)} %copy-done, bf16[1728,192]{1,0:T(8,128)(2,1)S(1)} %copy-done.1, bf16[1728,192]{1,0:T(8,128)(2,1)S(1)} %copy-done.2, ...), custom_call_target="tpu_custom_call" | custom-call | flops 1132462080 | bytes 14745600 | tf_op jit(solution)/shard_map/pallas_call | solution.py:108
  117.6 8.0 %shard_map.132 = (bf16[288,2560]{1,0:T(8,128)(2,1)}, f32[1728,2560]{1,0:T(8,128)}, f32[1728,2560]{1,0:T(8,128)}) custom-call(s32[1]{0:T(128)} %bitcast.place, bf16[1728,192]{1,0:T(8,128)(2,1)S(1)} %copy-done.3, bf16[1728,192]{1,0:T(8,128)(2,1)S(1)} %copy-done, bf16[1728,192]{1,0:T(8,128)(2,1)S(1)} %copy-done.1, ...), custom_call_target="tpu_custom_call", output_to_operand_aliasing={{1}: (12, {}), {2}: (13, {})} | custom-call | flops 1132462080 | bytes 14745600 | tf_op jit(solution)/shard_map/pallas_call | solution.py:108
  127.3 8.0 %shard_map.133 = (bf16[288,2560]{1,0:T(8,128)(2,1)}, f32[1728,2560]{1,0:T(8,128)}, f32[1728,2560]{1,0:T(8,128)}) custom-call(s32[1]{0:T(128)} %bitcast.place, bf16[1728,192]{1,0:T(8,128)(2,1)S(1)} %copy-done.3, bf16[1728,192]{1,0:T(8,128)(2,1)S(1)} %copy-done, bf16[1728,192]{1,0:T(8,128)(2,1)S(1)} %copy-done.1, ...), custom_call_target="tpu_custom_call", output_to_operand_aliasing={{1}: (12, {}), {2}: (13, {})} | custom-call | flops 1132462080 | bytes 14745600 | tf_op jit(solution)/shard_map/pallas_call | solution.py:108
  135.4 8.0 %shard_map.134 = (bf16[288,2560]{1,0:T(8,128)(2,1)}, f32[1728,2560]{1,0:T(8,128)}, f32[1728,2560]{1,0:T(8,128)}) custom-call(s32[1]{0:T(128)} %bitcast.place, bf16[1728,192]{1,0:T(8,128)(2,1)S(1)} %copy-done.3, bf16[1728,192]{1,0:T(8,128)(2,1)S(1)} %copy-done, bf16[1728,192]{1,0:T(8,128)(2,1)S(1)} %copy-done.1, ...), custom_call_target="tpu_custom_call", output_to_operand_aliasing={{1}: (12, {}), {2}: (13, {})} | custom-call | flops 1132462080 | bytes 14745600 | tf_op jit(solution)/shard_map/pallas_call | solution.py:108
  143.4 8.0 %shard_map.135 = (bf16[288,2560]{1,0:T(8,128)(2,1)}, f32[1728,2560]{1,0:T(8,128)}, f32[1728,2560]{1,0:T(8,128)}) custom-call(s32[1]{0:T(128)} %bitcast.place, bf16[1728,192]{1,0:T(8,128)(2,1)S(1)} %copy-done.3, bf16[1728,192]{1,0:T(8,128)(2,1)S(1)} %copy-done, bf16[1728,192]{1,0:T(8,128)(2,1)S(1)} %copy-done.1, ...), custom_call_target="tpu_custom_call", output_to_operand_aliasing={{1}: (12, {}), {2}: (13, {})} | custom-call | flops 1132462080 | bytes 14745600 | tf_op jit(solution)/shard_map/pallas_call | solution.py:108
  151.4 7.7 %shard_map.136 = (bf16[288,2560]{1,0:T(8,128)(2,1)S(1)}, f32[1728,2560]{1,0:T(8,128)}, f32[1728,2560]{1,0:T(8,128)}) custom-call(s32[1]{0:T(128)} %bitcast.place, bf16[1728,192]{1,0:T(8,128)(2,1)S(1)} %copy-done.3, bf16[1728,192]{1,0:T(8,128)(2,1)S(1)} %copy-done, bf16[1728,192]{1,0:T(8,128)(2,1)S(1)} %copy-done.1, ...), custom_call_target="tpu_custom_call", output_to_operand_aliasing={{1}: (12, {}), {2}: (13, {})} | custom-call | flops 1132462080 | bytes 14745600 | tf_op jit(solution)/shard_map/pallas_call | solution.py:108
  161.8 21.4 %collective-permute-done.17.refs_0_ = bf16[288,2560]{1,0:T(8,128)(2,1)S(1)} collective-permute-done((bf16[288,2560]{1,0:T(8,128)(2,1)}, bf16[288,2560]{1,0:T(8,128)(2,1)S(1)}, u32[]{:S(2)}, u32[]{:S(2)}) %collective-permute-start.17) | collective-permute-done | bytes 1474592 | tf_op jit(solution)/shard_map/ppermute | solution.py:196
  184.4 30.4 %collective-permute-done.14.rest_1_ = bf16[288,2560]{1,0:T(8,128)(2,1)} collective-permute-done((bf16[288,2560]{1,0:T(8,128)(2,1)}, bf16[288,2560]{1,0:T(8,128)(2,1)}, u32[]{:S(2)}, u32[]{:S(2)}) %collective-permute-start.14) | collective-permute-done | bytes 1474592 | tf_op jit(solution)/shard_map/ppermute | solution.py:196
  215.3 30.3 %collective-permute-done.11.rest_1_ = bf16[288,2560]{1,0:T(8,128)(2,1)} collective-permute-done((bf16[288,2560]{1,0:T(8,128)(2,1)}, bf16[288,2560]{1,0:T(8,128)(2,1)}, u32[]{:S(2)}, u32[]{:S(2)}) %collective-permute-start.11) | collective-permute-done | bytes 1474592 | tf_op jit(solution)/shard_map/ppermute | solution.py:196
  248.9 6.2 %shard_map.138 = (bf16[6912,2560]{1,0:T(8,128)(2,1)}, f32[8,128]{1,0:T(8,128)}) custom-call(s32[4]{0:T(128)S(1)} %pad_add_fusion.owners, bf16[288,2560]{1,0:T(8,128)(2,1)} %get-tuple-element.42.rest_0_, bf16[288,2560]{1,0:T(8,128)(2,1)} %collective-permute-done.20.rest_1_, bf16[288,2560]{1,0:T(8,128)(2,1)} %collective-permute-done.21.rest_2_, ...), custom_call_target="tpu_custom_call" | custom-call | bytes 11796480 | tf_op jit(solution)/shard_map/pallas_call | solution.py:156
  255.1 5.1 %shard_map.139 = (bf16[6912,2560]{1,0:T(8,128)(2,1)}, f32[8,128]{1,0:T(8,128)}) custom-call(s32[4]{0:T(128)S(1)} %pad_add_fusion.owners, bf16[288,2560]{1,0:T(8,128)(2,1)} %get-tuple-element.41.rest_0_, bf16[288,2560]{1,0:T(8,128)(2,1)S(1)} %copy-done.9, bf16[288,2560]{1,0:T(8,128)(2,1)} %collective-permute-done.18.rest_2_, ...), custom_call_target="tpu_custom_call", output_to_operand_aliasing={{0}: (5, {})} | custom-call | bytes 11796480 | tf_op jit(solution)/shard_map/pallas_call | solution.py:156
  260.6 5.9 %shard_map.140 = (bf16[6912,2560]{1,0:T(8,128)(2,1)}, f32[8,128]{1,0:T(8,128)}) custom-call(s32[4]{0:T(128)S(1)} %pad_add_fusion.owners, bf16[288,2560]{1,0:T(8,128)(2,1)} %get-tuple-element.40.rest_0_, bf16[288,2560]{1,0:T(8,128)(2,1)} %collective-permute-done.14.rest_1_, ...), custom_call_target="tpu_custom_call", output_to_operand_aliasing={{0}: (5, {})} | custom-call | bytes 11796480 | tf_op jit(solution)/shard_map/pallas_call | solution.py:156
  266.9 12.8 %collective-permute-done.25.rest_1_ = bf16[288,2560]{1,0:T(8,128)(2,1)} collective-permute-done((bf16[288,2560]{1,0:T(8,128)(2,1)}, bf16[288,2560]{1,0:T(8,128)(2,1)}, u32[]{:S(2)}, u32[]{:S(2)}) %collective-permute-start.25) | collective-permute-done | bytes 1474592 | tf_op jit(solution)/shard_map/ppermute | solution.py:196
  281.3 5.3 %shard_map.141 = (bf16[6912,2560]{1,0:T(8,128)(2,1)}, f32[8,128]{1,0:T(8,128)S(1)}) custom-call(s32[4]{0:T(128)S(1)} %pad_add_fusion.owners, bf16[288,2560]{1,0:T(8,128)(2,1)} %get-tuple-element.39.rest_0_, bf16[288,2560]{1,0:T(8,128)(2,1)} %collective-permute-done.11.rest_1_, ...), custom_call_target="tpu_custom_call", output_to_operand_aliasing={{0}: (5, {})} | custom-call | bytes 11796480 | tf_op jit(solution)/shard_map/pallas_call | solution.py:156
  287.2 23.9 %collective-permute-done.10.refs_0_ = bf16[288,2560]{1,0:T(8,128)(2,1)S(1)} collective-permute-done((bf16[288,2560]{1,0:T(8,128)(2,1)S(1)}, bf16[288,2560]{1,0:T(8,128)(2,1)S(1)}, u32[]{:S(2)}, u32[]{:S(2)}) %collective-permute-start.10) | collective-permute-done | bytes 1474592 | tf_op jit(solution)/shard_map/ppermute | solution.py:196
  313.3 5.9 %shard_map.143 = (bf16[6912,2560]{1,0:T(8,128)(2,1)}, f32[8,128]{1,0:T(8,128)}) custom-call(s32[4]{0:T(128)S(1)} %pad_add_fusion.owners, bf16[288,2560]{1,0:T(8,128)(2,1)} %get-tuple-element.47.rest_0_, bf16[288,2560]{1,0:T(8,128)(2,1)} %collective-permute-done.25.rest_1_, ...), custom_call_target="tpu_custom_call", output_to_operand_aliasing={{0}: (5, {})} | custom-call | bytes 11796480 | tf_op jit(solution)/shard_map/pallas_call | solution.py:156
  319.3 5.1 %shard_map.144 = (bf16[6912,2560]{1,0:T(8,128)(2,1)}, f32[8,128]{1,0:T(8,128)}) custom-call(s32[4]{0:T(128)S(1)} %pad_add_fusion.owners, bf16[288,2560]{1,0:T(8,128)(2,1)S(1)} %copy-done.5, bf16[288,2560]{1,0:T(8,128)(2,1)S(1)} %copy-done.7, bf16[288,2560]{1,0:T(8,128)(2,1)} %collective-permute-done.23.rest_2_, ...), custom_call_target="tpu_custom_call", output_to_operand_aliasing={{0}: (5, {})} | custom-call | bytes 11796480 | tf_op jit(solution)/shard_map/pallas_call | solution.py:156
  (102 shorter events, 32.4 us)
Async XLA Ops:
  0.7 31.3 %collective-permute-start = (bf16[96,6912]{1,0:T(8,128)(2,1)}, bf16[96,6912]{1,0:T(8,128)(2,1)S(1)}, u32[]{:S(2)}, u32[]{:S(2)}) collective-permute-start(bf16[96,6912]{1,0:T(8,128)(2,1)} %param.11), channel_id=1, source_target_pairs={{0,16},{16,0},{1,17},{17,1},{2,18},{18,2},{3,19},{19,3},{4,20},{20... | collective-permute-start | bytes 3981320 | tf_op jit(solution)/shard_map/ppermute | solution.py:231
  2.8 101.0 %collective-permute-start.9 = (bf16[192,2560]{1,0:T(8,128)(2,1)}, bf16[192,2560]{1,0:T(8,128)(2,1)}, u32[]{:S(2)}, u32[]{:S(2)}) collective-permute-start(bf16[192,2560]{1,0:T(8,128)(2,1)} %param.13), channel_id=1, source_target_pairs={{0,12},{4,0},{8,4},{12,8},{1,13},{5,1},{9,5},{13,9},{2,14},{6,2},{... | collective-permute-start | bytes 2949128 | tf_op jit(solution)/shard_map/ppermute | solution.py:248
  3.8 103.1 %collective-permute-start.7 = (bf16[192,2560]{1,0:T(8,128)(2,1)}, bf16[192,2560]{1,0:T(8,128)(2,1)}, u32[]{:S(2)}, u32[]{:S(2)}) collective-permute-start(bf16[192,2560]{1,0:T(8,128)(2,1)} %param.13), channel_id=1, source_target_pairs={{0,8},{4,12},{8,0},{12,4},{1,9},{5,13},{9,1},{13,5},{2,10},{6,14},... | collective-permute-start | bytes 2949128 | tf_op jit(solution)/shard_map/ppermute | solution.py:248
  41.6 22.6 %collective-permute-start.1 = (bf16[1728,192]{0,1:T(8,128)(2,1)}, bf16[1728,192]{0,1:T(8,128)(2,1)}, u32[]{:S(2)}, u32[]{:S(2)}) collective-permute-start(bf16[1728,192]{0,1:T(8,128)(2,1)} %copy.67), channel_id=1, source_target_pairs={{0,4},{4,8},{8,12},{12,0},{1,5},{5,9},{9,13},{13,1},{2,6},{6,10},{... | collective-permute-start | bytes 1990664 | tf_op jit(solution)/shard_map/ppermute | solution.py:247
  46.4 25.5 %collective-permute-start.2 = (bf16[1728,192]{0,1:T(8,128)(2,1)}, bf16[1728,192]{0,1:T(8,128)(2,1)}, u32[]{:S(2)}, u32[]{:S(2)}) collective-permute-start(bf16[1728,192]{0,1:T(8,128)(2,1)} %copy.68), channel_id=1, source_target_pairs={{0,8},{4,12},{8,0},{12,4},{1,9},{5,13},{9,1},{13,5},{2,10},{6,14},... | collective-permute-start | bytes 1990664 | tf_op jit(solution)/shard_map/ppermute | solution.py:247
  48.7 29.2 %collective-permute-start.3 = (bf16[1728,192]{0,1:T(8,128)(2,1)}, bf16[1728,192]{0,1:T(8,128)(2,1)}, u32[]{:S(2)}, u32[]{:S(2)}) collective-permute-start(bf16[1728,192]{0,1:T(8,128)(2,1)} %copy.69), channel_id=1, source_target_pairs={{0,12},{4,0},{8,4},{12,8},{1,13},{5,1},{9,5},{13,9},{2,14},{6,2},{... | collective-permute-start | bytes 1990664 | tf_op jit(solution)/shard_map/ppermute | solution.py:247
  64.2 44.2 %collective-permute-start.5 = (bf16[192,2560]{1,0:T(8,128)(2,1)}, bf16[192,2560]{1,0:T(8,128)(2,1)S(1)}, u32[]{:S(2)}, u32[]{:S(2)}) collective-permute-start(bf16[192,2560]{1,0:T(8,128)(2,1)} %param.13), channel_id=1, source_target_pairs={{0,4},{4,8},{8,12},{12,0},{1,5},{5,9},{9,13},{13,1},{2,6},{6,10},{... | collective-permute-start | bytes 2949128 | tf_op jit(solution)/shard_map/ppermute | solution.py:248
  80.3 18.7 %copy-start.15 = (f32[192]{0:T(256)S(1)}, f32[192]{0:T(256)}, u32[]{:S(2)}) copy-start(f32[192]{0:T(256)} %param.16) | copy-start | bytes 2308
  80.3 18.7 %copy-start.16 = (f32[192]{0:T(256)S(1)}, f32[192]{0:T(256)}, u32[]{:S(2)}) copy-start(f32[192]{0:T(256)} %param.15) | copy-start | bytes 2308
  80.3 18.7 %copy-start.17 = (f32[192]{0:T(256)S(1)}, f32[192]{0:T(256)}, u32[]{:S(2)}) copy-start(f32[192]{0:T(256)} %param.14) | copy-start | bytes 2308
  99.1 6.3 %collective-permute-start.8 = (f32[192]{0:T(256)S(1)}, f32[192]{0:T(256)S(1)}, u32[]{:S(2)}, u32[]{:S(2)}) collective-permute-start(f32[192]{0:T(256)S(1)} %negate_add_fusion), channel_id=1, source_target_pairs={{0,12},{4,0},{8,4},{12,8},{1,13},{5,1},{9,5},{13,9},{2,14},{6,2},{... | collective-permute-start | bytes 2312 | tf_op jit(solution)/shard_map/ppermute | solution.py:257
  102.2 4.7 %collective-permute-start.6 = (f32[192]{0:T(256)S(1)}, f32[192]{0:T(256)S(1)}, u32[]{:S(2)}, u32[]{:S(2)}) collective-permute-start(f32[192]{0:T(256)S(1)} %negate_add_fusion), channel_id=1, source_target_pairs={{0,8},{4,12},{8,0},{12,4},{1,9},{5,13},{9,1},{13,5},{2,10},{6,14},... | collective-permute-start | bytes 2312 | tf_op jit(solution)/shard_map/ppermute | solution.py:257
  103.8 4.7 %collective-permute-start.4 = (f32[192]{0:T(256)S(1)}, f32[192]{0:T(256)S(1)}, u32[]{:S(2)}, u32[]{:S(2)}) collective-permute-start(f32[192]{0:T(256)S(1)} %negate_add_fusion), channel_id=1, source_target_pairs={{0,4},{4,8},{8,12},{12,0},{1,5},{5,9},{9,13},{13,1},{2,6},{6,10},{... | collective-permute-start | bytes 2312 | tf_op jit(solution)/shard_map/ppermute | solution.py:257
  117.0 43.2 %collective-permute-start.20 = (bf16[288,2560]{1,0:T(8,128)(2,1)}, bf16[288,2560]{1,0:T(8,128)(2,1)}, u32[]{:S(2)}, u32[]{:S(2)}) collective-permute-start(bf16[288,2560]{1,0:T(8,128)(2,1)} %get-tuple-element.42.rest_0_), channel_id=1, source_target_pairs={{0,8},{4,12},{8,0},{12,4},{1,9},{5,13},{9,1},{13,5},{2,10},{6,14},... | collective-permute-start | bytes 4423688 | tf_op jit(solution)/shard_map/ppermute | solution.py:196
  117.2 43.5 %collective-permute-start.21 = (bf16[288,2560]{1,0:T(8,128)(2,1)}, bf16[288,2560]{1,0:T(8,128)(2,1)}, u32[]{:S(2)}, u32[]{:S(2)}) collective-permute-start(bf16[288,2560]{1,0:T(8,128)(2,1)} %get-tuple-element.42.rest_0_), channel_id=1, source_target_pairs={{0,4},{4,0},{8,12},{12,8},{1,5},{5,1},{9,13},{13,9},{2,6},{6,2},{1... | collective-permute-start | bytes 4423688 | tf_op jit(solution)/shard_map/ppermute | solution.py:205
  125.6 57.6 %collective-permute-start.17 = (bf16[288,2560]{1,0:T(8,128)(2,1)}, bf16[288,2560]{1,0:T(8,128)(2,1)S(1)}, u32[]{:S(2)}, u32[]{:S(2)}) collective-permute-start(bf16[288,2560]{1,0:T(8,128)(2,1)} %get-tuple-element.41.rest_0_), channel_id=1, source_target_pairs={{0,8},{4,12},{8,0},{12,4},{1,9},{5,13},{9,1},{13,5},{2,10},{6,14},... | collective-permute-start | bytes 4423688 | tf_op jit(solution)/shard_map/ppermute | solution.py:196
  126.5 57.9 %collective-permute-start.18 = (bf16[288,2560]{1,0:T(8,128)(2,1)}, bf16[288,2560]{1,0:T(8,128)(2,1)}, u32[]{:S(2)}, u32[]{:S(2)}) collective-permute-start(bf16[288,2560]{1,0:T(8,128)(2,1)} %get-tuple-element.41.rest_0_), channel_id=1, source_target_pairs={{0,4},{4,0},{8,12},{12,8},{1,5},{5,1},{9,13},{13,9},{2,6},{6,2},{1... | collective-permute-start | bytes 4423688 | tf_op jit(solution)/shard_map/ppermute | solution.py:205
  135.3 79.5 %collective-permute-start.14 = (bf16[288,2560]{1,0:T(8,128)(2,1)}, bf16[288,2560]{1,0:T(8,128)(2,1)}, u32[]{:S(2)}, u32[]{:S(2)}) collective-permute-start(bf16[288,2560]{1,0:T(8,128)(2,1)} %get-tuple-element.40.rest_0_), channel_id=1, source_target_pairs={{0,8},{4,12},{8,0},{12,4},{1,9},{5,13},{9,1},{13,5},{2,10},{6,14},... | collective-permute-start | bytes 4423688 | tf_op jit(solution)/shard_map/ppermute | solution.py:196
  160.2 54.6 %collective-permute-start.15 = (bf16[288,2560]{1,0:T(8,128)(2,1)}, bf16[288,2560]{1,0:T(8,128)(2,1)}, u32[]{:S(2)}, u32[]{:S(2)}) collective-permute-start(bf16[288,2560]{1,0:T(8,128)(2,1)} %get-tuple-element.40.rest_0_), channel_id=1, source_target_pairs={{0,4},{4,0},{8,12},{12,8},{1,5},{5,1},{9,13},{13,9},{2,6},{6,2},{1... | collective-permute-start | bytes 4423688 | tf_op jit(solution)/shard_map/ppermute | solution.py:205
  160.7 85.0 %collective-permute-start.11 = (bf16[288,2560]{1,0:T(8,128)(2,1)}, bf16[288,2560]{1,0:T(8,128)(2,1)}, u32[]{:S(2)}, u32[]{:S(2)}) collective-permute-start(bf16[288,2560]{1,0:T(8,128)(2,1)} %get-tuple-element.39.rest_0_), channel_id=1, source_target_pairs={{0,8},{4,12},{8,0},{12,4},{1,9},{5,13},{9,1},{13,5},{2,10},{6,14},... | collective-permute-start | bytes 4423688 | tf_op jit(solution)/shard_map/ppermute | solution.py:196
  183.2 62.9 %collective-permute-start.22 = (bf16[288,2560]{1,0:T(8,128)(2,1)}, bf16[288,2560]{1,0:T(8,128)(2,1)}, u32[]{:S(2)}, u32[]{:S(2)}) collective-permute-start(bf16[288,2560]{1,0:T(8,128)(2,1)} %collective-permute-done.20.rest_1_), channel_id=1, source_target_pairs={{0,4},{4,0},{8,12},{12,8},{1,5},{5,1},{9,13},{13,9},{2,6},{6,2},{1... | collective-permute-start | bytes 4423688 | tf_op jit(solution)/shard_map/ppermute | solution.py:205
  184.4 64.2 %copy-start.5 = (bf16[288,2560]{1,0:T(8,128)(2,1)S(1)}, bf16[288,2560]{1,0:T(8,128)(2,1)}, u32[]{:S(2)}) copy-start(bf16[288,2560]{1,0:T(8,128)(2,1)} %copy-done.4) | copy-start | bytes 4423684
  184.4 62.9 %collective-permute-start.19 = (bf16[288,2560]{1,0:T(8,128)(2,1)}, bf16[288,2560]{1,0:T(8,128)(2,1)S(1)}, u32[]{:S(2)}, u32[]{:S(2)}) collective-permute-start(bf16[288,2560]{1,0:T(8,128)(2,1)} %shard_map.137.rest_1_), channel_id=1, source_target_pairs={{0,4},{4,0},{8,12},{12,8},{1,5},{5,1},{9,13},{13,9},{2,6},{6,2},{1... | collective-permute-start | bytes 4423688 | tf_op jit(solution)/shard_map/ppermute | solution.py:205
  214.8 45.5 %collective-permute-start.16 = (bf16[288,2560]{1,0:T(8,128)(2,1)}, bf16[288,2560]{1,0:T(8,128)(2,1)}, u32[]{:S(2)}, u32[]{:S(2)}) collective-permute-start(bf16[288,2560]{1,0:T(8,128)(2,1)} %collective-permute-done.14.rest_1_), channel_id=1, source_target_pairs={{0,4},{4,0},{8,12},{12,8},{1,5},{5,1},{9,13},{13,9},{2,6},{6,2},{1... | collective-permute-start | bytes 4423688 | tf_op jit(solution)/shard_map/ppermute | solution.py:205
  214.8 51.8 %collective-permute-start.12 = (bf16[288,2560]{1,0:T(8,128)(2,1)}, bf16[288,2560]{1,0:T(8,128)(2,1)}, u32[]{:S(2)}, u32[]{:S(2)}) collective-permute-start(bf16[288,2560]{1,0:T(8,128)(2,1)} %get-tuple-element.39.rest_0_), channel_id=1, source_target_pairs={{0,4},{4,0},{8,12},{12,8},{1,5},{5,1},{9,13},{13,9},{2,6},{6,2},{1... | collective-permute-start | bytes 4423688 | tf_op jit(solution)/shard_map/ppermute | solution.py:205
  245.6 34.0 %collective-permute-start.25 = (bf16[288,2560]{1,0:T(8,128)(2,1)}, bf16[288,2560]{1,0:T(8,128)(2,1)}, u32[]{:S(2)}, u32[]{:S(2)}) collective-permute-start(bf16[288,2560]{1,0:T(8,128)(2,1)} %get-tuple-element.47.rest_0_), channel_id=1, source_target_pairs={{0,8},{4,12},{8,0},{12,4},{1,9},{5,13},{9,1},{13,5},{2,10},{6,14},... | collective-permute-start | bytes 4423688 | tf_op jit(solution)/shard_map/ppermute | solution.py:196
  246.1 35.2 %collective-permute-start.13 = (bf16[288,2560]{1,0:T(8,128)(2,1)}, bf16[288,2560]{1,0:T(8,128)(2,1)}, u32[]{:S(2)}, u32[]{:S(2)}) collective-permute-start(bf16[288,2560]{1,0:T(8,128)(2,1)} %collective-permute-done.11.rest_1_), channel_id=1, source_target_pairs={{0,4},{4,0},{8,12},{12,8},{1,5},{5,1},{9,13},{13,9},{2,6},{6,2},{1... | collective-permute-start | bytes 4423688 | tf_op jit(solution)/shard_map/ppermute | solution.py:205
  248.5 62.6 %collective-permute-start.10 = (bf16[288,2560]{1,0:T(8,128)(2,1)S(1)}, bf16[288,2560]{1,0:T(8,128)(2,1)S(1)}, u32[]{:S(2)}, u32[]{:S(2)}) collective-permute-start(bf16[288,2560]{1,0:T(8,128)(2,1)S(1)} %copy-done.5), channel_id=1, source_target_pairs={{0,8},{4,12},{8,0},{12,4},{1,9},{5,13},{9,1},{13,5},{2,10},{6,14},... | collective-permute-start | bytes 4423688 | tf_op jit(solution)/shard_map/ppermute | solution.py:196
  260.3 53.0 %collective-permute-start.26 = (bf16[288,2560]{1,0:T(8,128)(2,1)}, bf16[288,2560]{1,0:T(8,128)(2,1)}, u32[]{:S(2)}, u32[]{:S(2)}) collective-permute-start(bf16[288,2560]{1,0:T(8,128)(2,1)} %get-tuple-element.47.rest_0_), channel_id=1, source_target_pairs={{0,4},{4,0},{8,12},{12,8},{1,5},{5,1},{9,13},{13,9},{2,6},{6,2},{1... | collective-permute-start | bytes 4423688 | tf_op jit(solution)/shard_map/ppermute | solution.py:205
  266.6 52.6 %collective-permute-start.23 = (bf16[288,2560]{1,0:T(8,128)(2,1)S(1)}, bf16[288,2560]{1,0:T(8,128)(2,1)}, u32[]{:S(2)}, u32[]{:S(2)}) collective-permute-start(bf16[288,2560]{1,0:T(8,128)(2,1)S(1)} %copy-done.5), channel_id=1, source_target_pairs={{0,4},{4,0},{8,12},{12,8},{1,5},{5,1},{9,13},{13,9},{2,6},{6,2},{1... | collective-permute-start | bytes 4423688 | tf_op jit(solution)/shard_map/ppermute | solution.py:205
  279.6 33.6 %collective-permute-start.27 = (bf16[288,2560]{1,0:T(8,128)(2,1)}, bf16[288,2560]{1,0:T(8,128)(2,1)}, u32[]{:S(2)}, u32[]{:S(2)}) collective-permute-start(bf16[288,2560]{1,0:T(8,128)(2,1)} %collective-permute-done.25.rest_1_), channel_id=1, source_target_pairs={{0,4},{4,0},{8,12},{12,8},{1,5},{5,1},{9,13},{13,9},{2,6},{6,2},{1... | collective-permute-start | bytes 4423688 | tf_op jit(solution)/shard_map/ppermute | solution.py:205
  312.3 7.0 %collective-permute-start.24 = (bf16[288,2560]{1,0:T(8,128)(2,1)}, bf16[288,2560]{1,0:T(8,128)(2,1)S(1)}, u32[]{:S(2)}, u32[]{:S(2)}) collective-permute-start(bf16[288,2560]{1,0:T(8,128)(2,1)} %shard_map.142.rest_1_), channel_id=1, source_target_pairs={{0,4},{4,0},{8,12},{12,8},{1,5},{5,1},{9,13},{13,9},{2,6},{6,2},{1... | collective-permute-start | bytes 4423688 | tf_op jit(solution)/shard_map/ppermute | solution.py:205
  (15 other events, 52.6 us)

commit v4 on v3

--- a/solution.py
+++ b/solution.py
@@ -259,7 +259,7 @@
     for here, block in zip(coeffs, right):
         weighted.append((here[:, None] * block.astype(jnp.float32)).astype(jnp.bfloat16))
 
-    chunks = max(n for n in range(1, 7) if shard_rows % (16 * n) == 0)
+    chunks = max(n for n in range(1, 10) if shard_rows % (16 * n) == 0)
     rows = shard_rows // chunks
     tile = rows // 2 if rows % 32 == 0 else rows
     where_am_i = me.reshape(1).astype(jnp.int32)

time: 325 us -> 330 us (1.015)
  waiting for transfers between devices: 150 us -> 133 us
  Pallas kernels: 81.3 us -> 91.7 us
  local copies, waits for them, and re-layouts: 23.8 us -> 30.3 us
    ppermute x6 -> x9, waiting for transfers between devices: 119 us -> 104 us  [send_far(): lax.ppermute(chunk, 'dp', [(i, (i + hop) % count) for i in range(count)])]
    unnamed x39 -> x99, local copies, waits for them, and re-layouts: 8.24 us -> 14.7 us
    pallas_call x6 -> x9, Pallas kernels: 47.6 us -> 53 us  [update_rows(): pl.pallas_call(functools.partial(update_kernel, count), grid_spec=pltpu.P...]
    pallas_call x6 -> x9, Pallas kernels: 33.7 us -> 38.7 us  [place_rows(): pl.pallas_call(functools.partial(place_kernel, count, shard_rows, start),...]
    ppermute x6 -> x9, starting transfers between devices: 3.04 us -> 6.5 us  [send_far(): lax.ppermute(chunk, 'dp', [(i, (i + hop) % count) for i in range(count)])]
    ppermute x12 -> x18, starting transfers between devices: 6.69 us -> 5.85 us  [send_near(): lax.ppermute(piece, 'dp', swap)]
  transfers between devices with their start and end apart: 28 -> 37, of which waited for: 8 -> 11; matrix products, arithmetic and copies ran while one was open for 14% -> 14% of each run, Pallas kernels for 21% -> 23%
where the time goes in v4:
time: 330 us
  waiting for transfers between devices  133 us (40%)
  Pallas kernels  91.7 us (28%)
  local copies, waits for them, and re-layouts  30.3 us (9%)
  starting transfers between devices  25.9 us (8%)
  blocking collectives  18.7 us (6%)
  matrix products  15.1 us (5%)
  other arithmetic  13.6 us (4%)
    ppermute x9, waiting for transfers between devices, send_far(): lax.ppermute(chunk, 'dp', [(i, (i + hop) % count) for i in range(count)])  104 us
    pallas_call x9, Pallas kernels, update_rows(): pl.pallas_call(functools.partial(update_kernel, count), grid_spec=pltpu.P...  53 us
    pallas_call x9, Pallas kernels, place_rows(): pl.pallas_call(functools.partial(place_kernel, count, shard_rows, start),...  38.7 us
    ppermute x1, waiting for transfers between devices, on_device(): halves.append(lax.ppermute(activations, 'section', shift))  21 us
    psum x1, blocking collectives, on_device(): new_logp = logp_rest + lax.psum(score_share, ('section', 'mp'))  18.7 us
    dot_general x1, matrix products, on_device(): layer_out = jnp.dot(gathered, weight, preferred_element_type=jnp.float32)  15.1 us
    unnamed x99, local copies, waits for them, and re-layouts  14.7 us
    ppermute x3, waiting for transfers between devices, on_device(): lax.ppermute(block_for(lax.rem(me + hop, count)), 'dp', shifts[hop - 1])  7.73 us
  transfers between devices with their start and end apart: 37, of which 11 were waited for; matrix products, arithmetic and copies ran while one was open for 14% of the time, Pallas kernels for 23%

profile of v4, /device:TPU:1, one launch (start us, length us, event | category | flops | bytes accessed | tf_op | source)
XLA Modules:
  0.0 329.5 jit_solution(9304912569428848706)
XLA Ops:
  10.9 21.0 %collective-permute-done = bf16[96,6912]{1,0:T(8,128)(2,1)S(1)} collective-permute-done((bf16[96,6912]{1,0:T(8,128)(2,1)}, bf16[96,6912]{1,0:T(8,128)(2,1)S(1)}, u32[]{:S(2)}, u32[]{:S(2)}) %collective-permute-start) | collective-permute-done | bytes 1327136 | tf_op jit(solution)/shard_map/ppermute | solution.py:231
  35.8 3.4 %fusion.9 = (bf16[1728,192]{1,0:T(8,128)(2,1)}, bf16[1728,192]{1,0:T(8,128)(2,1)}, bf16[1728,192]{1,0:T(8,128)(2,1)}, bf16[1728,192]{1,0:T(8,128)(2,1)}) fusion(s32[]{:T(128)S(6)} %select_n.87, bf16[96,6912]{0,1:T(8,128)(2,1)S(1)} %get-tuple-element.86, bf16[96,6912]{0,1:T(8,128)(2,1)S(1)} %get-tuple-element.85, s32[]{:T(128)S(6)} %select_n.84, ...), kind=kLoop, calls=%fused_computation.25 | loop fusion | flops 5308416 | bytes 5308432 | tf_op jit(solution)/shard_map/dynamic_slice | solution.py:242
  49.0 15.1 %fusion.1 = f32[192]{0:T(256)} fusion(bf16[192,2560]{1,0:T(8,128)(2,1)} %param.13, bf16[6912,2560]{1,0:T(8,128)(2,1)} %refs_8_.17, bf16[96,6912]{0,1:T(8,128)(2,1)S(1)} %get-tuple-element.85, bf16[96,6912]{0,1:T(8,128)(2,1)S(1)} %get-tuple-element.86), kind=kOutput, calls=%fused_computation.17 | convolution fusion | flops 6801555456 | bytes 39027456 | tf_op jit(solution)/shard_map/dot_general | solution.py:250
  67.9 3.9 %collective-permute-done.2 = bf16[1728,192]{0,1:T(8,128)(2,1)} collective-permute-done((bf16[1728,192]{0,1:T(8,128)(2,1)}, bf16[1728,192]{0,1:T(8,128)(2,1)}, u32[]{:S(2)}, u32[]{:S(2)}) %collective-permute-start.2) | collective-permute-done | bytes 663584 | tf_op jit(solution)/shard_map/ppermute | solution.py:247
  74.2 3.8 %collective-permute-done.3 = bf16[1728,192]{0,1:T(8,128)(2,1)} collective-permute-done((bf16[1728,192]{0,1:T(8,128)(2,1)}, bf16[1728,192]{0,1:T(8,128)(2,1)}, u32[]{:S(2)}, u32[]{:S(2)}) %collective-permute-start.3) | collective-permute-done | bytes 663584 | tf_op jit(solution)/shard_map/ppermute | solution.py:247
  80.3 18.7 %psum.7 = f32[192]{0:T(256)S(1)} all-reduce(f32[192]{0:T(256)} %bitcast.40), channel_id=1, replica_groups=mesh['section'=2,'dp'=4,'mp'=4] {'section','mp'}, use_global_device_ids=true, to_apply=%region_2.0 | all-reduce | flops 192 | bytes 1536 | tf_op jit(solution)/shard_map/psum | solution.py:253
  108.7 5.8 %shard_map.131 = (bf16[192,2560]{1,0:T(8,128)(2,1)S(1)}, f32[1728,2560]{1,0:T(8,128)}, f32[1728,2560]{1,0:T(8,128)}) custom-call(s32[1]{0:T(128)} %bitcast.place, bf16[1728,192]{1,0:T(8,128)(2,1)S(1)} %copy-done.3, bf16[1728,192]{1,0:T(8,128)(2,1)S(1)} %copy-done, bf16[1728,192]{1,0:T(8,128)(2,1)S(1)} %copy-done.1, bf16[1728,192]{1,0:T(8,128)(2,1)S(1)} %copy-done.2, ...), custom_call_target="tpu_custom_call" | custom-call | flops 754974720 | bytes 9830400 | tf_op jit(solution)/shard_map/pallas_call | solution.py:108
  114.4 6.1 %shard_map.132 = (bf16[192,2560]{1,0:T(8,128)(2,1)S(1)}, f32[1728,2560]{1,0:T(8,128)}, f32[1728,2560]{1,0:T(8,128)}) custom-call(s32[1]{0:T(128)} %bitcast.place, bf16[1728,192]{1,0:T(8,128)(2,1)S(1)} %copy-done.3, bf16[1728,192]{1,0:T(8,128)(2,1)S(1)} %copy-done, bf16[1728,192]{1,0:T(8,128)(2,1)S(1)} %copy-done.1, ...), custom_call_target="tpu_custom_call", output_to_operand_aliasing={{1}: (12, {}), {2}: (13, {})} | custom-call | flops 754974720 | bytes 9830400 | tf_op jit(solution)/shard_map/pallas_call | solution.py:108
  122.5 5.7 %shard_map.133 = (bf16[192,2560]{1,0:T(8,128)(2,1)S(1)}, f32[1728,2560]{1,0:T(8,128)}, f32[1728,2560]{1,0:T(8,128)}) custom-call(s32[1]{0:T(128)} %bitcast.place, bf16[1728,192]{1,0:T(8,128)(2,1)S(1)} %copy-done.3, bf16[1728,192]{1,0:T(8,128)(2,1)S(1)} %copy-done, bf16[1728,192]{1,0:T(8,128)(2,1)S(1)} %copy-done.1, ...), custom_call_target="tpu_custom_call", output_to_operand_aliasing={{1}: (12, {}), {2}: (13, {})} | custom-call | flops 754974720 | bytes 9830400 | tf_op jit(solution)/shard_map/pallas_call | solution.py:108
  128.8 15.5 %collective-permute-done.26.refs_0_ = bf16[192,2560]{1,0:T(8,128)(2,1)S(1)} collective-permute-done((bf16[192,2560]{1,0:T(8,128)(2,1)S(1)}, bf16[192,2560]{1,0:T(8,128)(2,1)S(1)}, u32[]{:S(2)}, u32[]{:S(2)}) %collective-permute-start.26) | collective-permute-done | bytes 983072 | tf_op jit(solution)/shard_map/ppermute | solution.py:196
  144.3 6.1 %shard_map.134 = (bf16[192,2560]{1,0:T(8,128)(2,1)S(1)}, f32[1728,2560]{1,0:T(8,128)}, f32[1728,2560]{1,0:T(8,128)}) custom-call(s32[1]{0:T(128)} %bitcast.place, bf16[1728,192]{1,0:T(8,128)(2,1)S(1)} %copy-done.3, bf16[1728,192]{1,0:T(8,128)(2,1)S(1)} %copy-done, bf16[1728,192]{1,0:T(8,128)(2,1)S(1)} %copy-done.1, ...), custom_call_target="tpu_custom_call", output_to_operand_aliasing={{1}: (12, {}), {2}: (13, {})} | custom-call | flops 754974720 | bytes 9830400 | tf_op jit(solution)/shard_map/pallas_call | solution.py:108
  150.4 15.0 %collective-permute-done.29.rest_1_ = bf16[192,2560]{1,0:T(8,128)(2,1)S(1)} collective-permute-done((bf16[192,2560]{1,0:T(8,128)(2,1)S(1)}, bf16[192,2560]{1,0:T(8,128)(2,1)S(1)}, u32[]{:S(2)}, u32[]{:S(2)}) %collective-permute-start.29) | collective-permute-done | bytes 983072 | tf_op jit(solution)/shard_map/ppermute | solution.py:196
  166.8 5.9 %shard_map.135 = (bf16[192,2560]{1,0:T(8,128)(2,1)}, f32[1728,2560]{1,0:T(8,128)}, f32[1728,2560]{1,0:T(8,128)}) custom-call(s32[1]{0:T(128)} %bitcast.place, bf16[1728,192]{1,0:T(8,128)(2,1)S(1)} %copy-done.3, bf16[1728,192]{1,0:T(8,128)(2,1)S(1)} %copy-done, bf16[1728,192]{1,0:T(8,128)(2,1)S(1)} %copy-done.1, ...), custom_call_target="tpu_custom_call", output_to_operand_aliasing={{1}: (12, {}), {2}: (13, {})} | custom-call | flops 754974720 | bytes 9830400 | tf_op jit(solution)/shard_map/pallas_call | solution.py:108
  172.8 6.0 %shard_map.136 = (bf16[192,2560]{1,0:T(8,128)(2,1)}, f32[1728,2560]{1,0:T(8,128)}, f32[1728,2560]{1,0:T(8,128)}) custom-call(s32[1]{0:T(128)} %bitcast.place, bf16[1728,192]{1,0:T(8,128)(2,1)S(1)} %copy-done.3, bf16[1728,192]{1,0:T(8,128)(2,1)S(1)} %copy-done, bf16[1728,192]{1,0:T(8,128)(2,1)S(1)} %copy-done.1, ...), custom_call_target="tpu_custom_call", output_to_operand_aliasing={{1}: (12, {}), {2}: (13, {})} | custom-call | flops 754974720 | bytes 9830400 | tf_op jit(solution)/shard_map/pallas_call | solution.py:108
  179.2 7.2 %collective-permute-done.23.rest_1_ = bf16[192,2560]{1,0:T(8,128)(2,1)S(1)} collective-permute-done((bf16[192,2560]{1,0:T(8,128)(2,1)S(1)}, bf16[192,2560]{1,0:T(8,128)(2,1)S(1)}, u32[]{:S(2)}, u32[]{:S(2)}) %collective-permute-start.23) | collective-permute-done | bytes 983072 | tf_op jit(solution)/shard_map/ppermute | solution.py:196
  187.6 5.9 %shard_map.137 = (bf16[192,2560]{1,0:T(8,128)(2,1)}, f32[1728,2560]{1,0:T(8,128)}, f32[1728,2560]{1,0:T(8,128)}) custom-call(s32[1]{0:T(128)} %bitcast.place, bf16[1728,192]{1,0:T(8,128)(2,1)S(1)} %copy-done.3, bf16[1728,192]{1,0:T(8,128)(2,1)S(1)} %copy-done, bf16[1728,192]{1,0:T(8,128)(2,1)S(1)} %copy-done.1, ...), custom_call_target="tpu_custom_call", output_to_operand_aliasing={{1}: (12, {}), {2}: (13, {})} | custom-call | flops 754974720 | bytes 9830400 | tf_op jit(solution)/shard_map/pallas_call | solution.py:108
  193.6 14.0 %collective-permute-done.20.rest_1_ = bf16[192,2560]{1,0:T(8,128)(2,1)S(1)} collective-permute-done((bf16[192,2560]{1,0:T(8,128)(2,1)S(1)}, bf16[192,2560]{1,0:T(8,128)(2,1)S(1)}, u32[]{:S(2)}, u32[]{:S(2)}) %collective-permute-start.20) | collective-permute-done | bytes 983072 | tf_op jit(solution)/shard_map/ppermute | solution.py:196
  208.7 5.7 %shard_map.138 = (bf16[192,2560]{1,0:T(8,128)(2,1)S(1)}, f32[1728,2560]{1,0:T(8,128)}, f32[1728,2560]{1,0:T(8,128)}) custom-call(s32[1]{0:T(128)} %bitcast.place, bf16[1728,192]{1,0:T(8,128)(2,1)S(1)} %copy-done.3, bf16[1728,192]{1,0:T(8,128)(2,1)S(1)} %copy-done, bf16[1728,192]{1,0:T(8,128)(2,1)S(1)} %copy-done.1, ...), custom_call_target="tpu_custom_call", output_to_operand_aliasing={{1}: (12, {}), {2}: (13, {})} | custom-call | flops 754974720 | bytes 9830400 | tf_op jit(solution)/shard_map/pallas_call | solution.py:108
  215.4 5.8 %shard_map.139 = (bf16[192,2560]{1,0:T(8,128)(2,1)S(1)}, f32[1728,2560]{1,0:T(8,128)}, f32[1728,2560]{1,0:T(8,128)}) custom-call(s32[1]{0:T(128)} %bitcast.place, bf16[1728,192]{1,0:T(8,128)(2,1)S(1)} %copy-done.3, bf16[1728,192]{1,0:T(8,128)(2,1)S(1)} %copy-done, bf16[1728,192]{1,0:T(8,128)(2,1)S(1)} %copy-done.1, ...), custom_call_target="tpu_custom_call", output_to_operand_aliasing={{1}: (12, {}), {2}: (13, {})} | custom-call | flops 754974720 | bytes 9830400 | tf_op jit(solution)/shard_map/pallas_call | solution.py:108
  222.2 6.5 %collective-permute-done.17.rest_1_ = bf16[192,2560]{1,0:T(8,128)(2,1)} collective-permute-done((bf16[192,2560]{1,0:T(8,128)(2,1)}, bf16[192,2560]{1,0:T(8,128)(2,1)}, u32[]{:S(2)}, u32[]{:S(2)}) %collective-permute-start.17) | collective-permute-done | bytes 983072 | tf_op jit(solution)/shard_map/ppermute | solution.py:196
  229.2 20.5 %collective-permute-done.14.rest_1_ = bf16[192,2560]{1,0:T(8,128)(2,1)} collective-permute-done((bf16[192,2560]{1,0:T(8,128)(2,1)}, bf16[192,2560]{1,0:T(8,128)(2,1)}, u32[]{:S(2)}, u32[]{:S(2)}) %collective-permute-start.14) | collective-permute-done | bytes 983072 | tf_op jit(solution)/shard_map/ppermute | solution.py:196
  250.3 19.9 %collective-permute-done.11.rest_1_ = bf16[192,2560]{1,0:T(8,128)(2,1)} collective-permute-done((bf16[192,2560]{1,0:T(8,128)(2,1)}, bf16[192,2560]{1,0:T(8,128)(2,1)}, u32[]{:S(2)}, u32[]{:S(2)}) %collective-permute-start.11) | collective-permute-done | bytes 983072 | tf_op jit(solution)/shard_map/ppermute | solution.py:196
  281.5 4.3 %shard_map.141 = (bf16[6912,2560]{1,0:T(8,128)(2,1)}, f32[8,128]{1,0:T(8,128)}) custom-call(s32[4]{0:T(128)S(1)} %pad_add_fusion.owners, bf16[192,2560]{1,0:T(8,128)(2,1)S(1)} %copy-done.11, bf16[192,2560]{1,0:T(8,128)(2,1)S(1)} %copy-done.14, bf16[192,2560]{1,0:T(8,128)(2,1)S(1)} %copy-done.16, bf16[192,2560]{1,0:T(8,128)(2,1)S(1)} %copy-done.18), custom_call_target="tpu_custom_call" | custom-call | bytes 7864320 | tf_op jit(solution)/shard_map/pallas_call | solution.py:156
  285.9 4.4 %shard_map.142 = (bf16[6912,2560]{1,0:T(8,128)(2,1)}, f32[8,128]{1,0:T(8,128)}) custom-call(s32[4]{0:T(128)S(1)} %pad_add_fusion.owners, bf16[192,2560]{1,0:T(8,128)(2,1)S(1)} %copy-done.20, bf16[192,2560]{1,0:T(8,128)(2,1)S(1)} %copy-done.7, bf16[192,2560]{1,0:T(8,128)(2,1)S(1)} %copy-done.24, ...), custom_call_target="tpu_custom_call", output_to_operand_aliasing={{0}: (5, {})} | custom-call | bytes 7864320 | tf_op jit(solution)/shard_map/pallas_call | solution.py:156
  290.4 4.3 %shard_map.143 = (bf16[6912,2560]{1,0:T(8,128)(2,1)}, f32[8,128]{1,0:T(8,128)}) custom-call(s32[4]{0:T(128)S(1)} %pad_add_fusion.owners, bf16[192,2560]{1,0:T(8,128)(2,1)S(1)} %copy-done.22, bf16[192,2560]{1,0:T(8,128)(2,1)S(1)} %copy-done.26, bf16[192,2560]{1,0:T(8,128)(2,1)S(1)} %copy-done.32, ...), custom_call_target="tpu_custom_call", output_to_operand_aliasing={{0}: (5, {})} | custom-call | bytes 7864320 | tf_op jit(solution)/shard_map/pallas_call | solution.py:156
  294.8 4.3 %shard_map.144 = (bf16[6912,2560]{1,0:T(8,128)(2,1)}, f32[8,128]{1,0:T(8,128)}) custom-call(s32[4]{0:T(128)S(1)} %pad_add_fusion.owners, bf16[192,2560]{1,0:T(8,128)(2,1)S(1)} %copy-done.30, bf16[192,2560]{1,0:T(8,128)(2,1)S(1)} %copy-done.34, bf16[192,2560]{1,0:T(8,128)(2,1)S(1)} %copy-done.36, ...), custom_call_target="tpu_custom_call", output_to_operand_aliasing={{0}: (5, {})} | custom-call | bytes 7864320 | tf_op jit(solution)/shard_map/pallas_call | solution.py:156
  299.2 4.3 %shard_map.145 = (bf16[6912,2560]{1,0:T(8,128)(2,1)}, f32[8,128]{1,0:T(8,128)}) custom-call(s32[4]{0:T(128)S(1)} %pad_add_fusion.owners, bf16[192,2560]{1,0:T(8,128)(2,1)} %get-tuple-element.59.rest_0_, bf16[192,2560]{1,0:T(8,128)(2,1)} %collective-permute-done.17.rest_1_, ...), custom_call_target="tpu_custom_call", output_to_operand_aliasing={{0}: (5, {})} | custom-call | bytes 7864320 | tf_op jit(solution)/shard_map/pallas_call | solution.py:156
  303.9 4.3 %shard_map.146 = (bf16[6912,2560]{1,0:T(8,128)(2,1)}, f32[8,128]{1,0:T(8,128)}) custom-call(s32[4]{0:T(128)S(1)} %pad_add_fusion.owners, bf16[192,2560]{1,0:T(8,128)(2,1)} %get-tuple-element.58.rest_0_, bf16[192,2560]{1,0:T(8,128)(2,1)} %collective-permute-done.14.rest_1_, ...), custom_call_target="tpu_custom_call", output_to_operand_aliasing={{0}: (5, {})} | custom-call | bytes 7864320 | tf_op jit(solution)/shard_map/pallas_call | solution.py:156
  308.8 3.7 %shard_map.147 = (bf16[6912,2560]{1,0:T(8,128)(2,1)}, f32[8,128]{1,0:T(8,128)S(1)}) custom-call(s32[4]{0:T(128)S(1)} %pad_add_fusion.owners, bf16[192,2560]{1,0:T(8,128)(2,1)} %get-tuple-element.57.rest_0_, bf16[192,2560]{1,0:T(8,128)(2,1)} %collective-permute-done.11.rest_1_, ...), custom_call_target="tpu_custom_call", output_to_operand_aliasing={{0}: (5, {})} | custom-call | bytes 7864320 | tf_op jit(solution)/shard_map/pallas_call | solution.py:156
  313.2 5.3 %collective-permute-done.10.refs_0_ = bf16[192,2560]{1,0:T(8,128)(2,1)S(1)} collective-permute-done((bf16[192,2560]{1,0:T(8,128)(2,1)}, bf16[192,2560]{1,0:T(8,128)(2,1)S(1)}, u32[]{:S(2)}, u32[]{:S(2)}) %collective-permute-start.10) | collective-permute-done | bytes 983072 | tf_op jit(solution)/shard_map/ppermute | solution.py:196
  320.4 4.7 %shard_map.149 = (bf16[6912,2560]{1,0:T(8,128)(2,1)}, f32[8,128]{1,0:T(8,128)}) custom-call(s32[4]{0:T(128)S(1)} %pad_add_fusion.owners, bf16[192,2560]{1,0:T(8,128)(2,1)S(1)} %copy-done.28, bf16[192,2560]{1,0:T(8,128)(2,1)} %collective-permute-done.34.rest_1_, bf16[192,2560]{1,0:T(8,128)(2,1)} %collective-permute-done.35.rest_2_, ...), custom_call_target="tpu_custom_call", output_to_operand_aliasing={{0}: (5, {})} | custom-call | bytes 7864320 | tf_op jit(solution)/shard_map/pallas_call | solution.py:156
  325.1 4.3 %shard_map.150 = (bf16[6912,2560]{1,0:T(8,128)(2,1)}, f32[8,128]{1,0:T(8,128)}) custom-call(s32[4]{0:T(128)S(1)} %pad_add_fusion.owners, bf16[192,2560]{1,0:T(8,128)(2,1)S(1)} %copy-done.5, bf16[192,2560]{1,0:T(8,128)(2,1)S(1)} %copy-done.9, bf16[192,2560]{1,0:T(8,128)(2,1)} %collective-permute-done.32.rest_2_, ...), custom_call_target="tpu_custom_call", output_to_operand_aliasing={{0}: (5, {})} | custom-call | bytes 7864320 | tf_op jit(solution)/shard_map/pallas_call | solution.py:156
  (186 shorter events, 66.4 us)
Async XLA Ops:
  0.6 31.3 %collective-permute-start = (bf16[96,6912]{1,0:T(8,128)(2,1)}, bf16[96,6912]{1,0:T(8,128)(2,1)S(1)}, u32[]{:S(2)}, u32[]{:S(2)}) collective-permute-start(bf16[96,6912]{1,0:T(8,128)(2,1)} %param.11), channel_id=1, source_target_pairs={{0,16},{16,0},{1,17},{17,1},{2,18},{18,2},{3,19},{19,3},{4,20},{20... | collective-permute-start | bytes 3981320 | tf_op jit(solution)/shard_map/ppermute | solution.py:231
  2.8 101.0 %collective-permute-start.9 = (bf16[192,2560]{1,0:T(8,128)(2,1)}, bf16[192,2560]{1,0:T(8,128)(2,1)}, u32[]{:S(2)}, u32[]{:S(2)}) collective-permute-start(bf16[192,2560]{1,0:T(8,128)(2,1)} %param.13), channel_id=1, source_target_pairs={{0,12},{4,0},{8,4},{12,8},{1,13},{5,1},{9,5},{13,9},{2,14},{6,2},{... | collective-permute-start | bytes 2949128 | tf_op jit(solution)/shard_map/ppermute | solution.py:248
  3.7 103.2 %collective-permute-start.7 = (bf16[192,2560]{1,0:T(8,128)(2,1)}, bf16[192,2560]{1,0:T(8,128)(2,1)}, u32[]{:S(2)}, u32[]{:S(2)}) collective-permute-start(bf16[192,2560]{1,0:T(8,128)(2,1)} %param.13), channel_id=1, source_target_pairs={{0,8},{4,12},{8,0},{12,4},{1,9},{5,13},{9,1},{13,5},{2,10},{6,14},... | collective-permute-start | bytes 2949128 | tf_op jit(solution)/shard_map/ppermute | solution.py:248
  41.6 22.6 %collective-permute-start.1 = (bf16[1728,192]{0,1:T(8,128)(2,1)}, bf16[1728,192]{0,1:T(8,128)(2,1)}, u32[]{:S(2)}, u32[]{:S(2)}) collective-permute-start(bf16[1728,192]{0,1:T(8,128)(2,1)} %copy.85), channel_id=1, source_target_pairs={{0,4},{4,8},{8,12},{12,0},{1,5},{5,9},{9,13},{13,1},{2,6},{6,10},{... | collective-permute-start | bytes 1990664 | tf_op jit(solution)/shard_map/ppermute | solution.py:247
  46.3 25.5 %collective-permute-start.2 = (bf16[1728,192]{0,1:T(8,128)(2,1)}, bf16[1728,192]{0,1:T(8,128)(2,1)}, u32[]{:S(2)}, u32[]{:S(2)}) collective-permute-start(bf16[1728,192]{0,1:T(8,128)(2,1)} %copy.86), channel_id=1, source_target_pairs={{0,8},{4,12},{8,0},{12,4},{1,9},{5,13},{9,1},{13,5},{2,10},{6,14},... | collective-permute-start | bytes 1990664 | tf_op jit(solution)/shard_map/ppermute | solution.py:247
  48.7 29.3 %collective-permute-start.3 = (bf16[1728,192]{0,1:T(8,128)(2,1)}, bf16[1728,192]{0,1:T(8,128)(2,1)}, u32[]{:S(2)}, u32[]{:S(2)}) collective-permute-start(bf16[1728,192]{0,1:T(8,128)(2,1)} %copy.87), channel_id=1, source_target_pairs={{0,12},{4,0},{8,4},{12,8},{1,13},{5,1},{9,5},{13,9},{2,14},{6,2},{... | collective-permute-start | bytes 1990664 | tf_op jit(solution)/shard_map/ppermute | solution.py:247
  64.2 44.2 %collective-permute-start.5 = (bf16[192,2560]{1,0:T(8,128)(2,1)}, bf16[192,2560]{1,0:T(8,128)(2,1)S(1)}, u32[]{:S(2)}, u32[]{:S(2)}) collective-permute-start(bf16[192,2560]{1,0:T(8,128)(2,1)} %param.13), channel_id=1, source_target_pairs={{0,4},{4,8},{8,12},{12,0},{1,5},{5,9},{9,13},{13,1},{2,6},{6,10},{... | collective-permute-start | bytes 2949128 | tf_op jit(solution)/shard_map/ppermute | solution.py:248
  120.5 23.8 %collective-permute-start.26 = (bf16[192,2560]{1,0:T(8,128)(2,1)S(1)}, bf16[192,2560]{1,0:T(8,128)(2,1)S(1)}, u32[]{:S(2)}, u32[]{:S(2)}) collective-permute-start(bf16[192,2560]{1,0:T(8,128)(2,1)S(1)} %get-tuple-element.62.rest_0_), channel_id=1, source_target_pairs={{0,8},{4,12},{8,0},{12,4},{1,9},{5,13},{9,1},{13,5},{2,10},{6,14},... | collective-permute-start | bytes 2949128 | tf_op jit(solution)/shard_map/ppermute | solution.py:196
  121.0 44.4 %collective-permute-start.29 = (bf16[192,2560]{1,0:T(8,128)(2,1)S(1)}, bf16[192,2560]{1,0:T(8,128)(2,1)S(1)}, u32[]{:S(2)}, u32[]{:S(2)}) collective-permute-start(bf16[192,2560]{1,0:T(8,128)(2,1)S(1)} %get-tuple-element.63.rest_0_), channel_id=1, source_target_pairs={{0,8},{4,12},{8,0},{12,4},{1,9},{5,13},{9,1},{13,5},{2,10},{6,14},... | collective-permute-start | bytes 2949128 | tf_op jit(solution)/shard_map/ppermute | solution.py:196
  122.0 43.6 %collective-permute-start.30 = (bf16[192,2560]{1,0:T(8,128)(2,1)S(1)}, bf16[192,2560]{1,0:T(8,128)(2,1)S(1)}, u32[]{:S(2)}, u32[]{:S(2)}) collective-permute-start(bf16[192,2560]{1,0:T(8,128)(2,1)S(1)} %get-tuple-element.63.rest_0_), channel_id=1, source_target_pairs={{0,4},{4,0},{8,12},{12,8},{1,5},{5,1},{9,13},{13,9},{2,6},{6,2},{1... | collective-permute-start | bytes 2949128 | tf_op jit(solution)/shard_map/ppermute | solution.py:205
  122.0 56.7 %collective-permute-start.27 = (bf16[192,2560]{1,0:T(8,128)(2,1)S(1)}, bf16[192,2560]{1,0:T(8,128)(2,1)S(1)}, u32[]{:S(2)}, u32[]{:S(2)}) collective-permute-start(bf16[192,2560]{1,0:T(8,128)(2,1)S(1)} %get-tuple-element.62.rest_0_), channel_id=1, source_target_pairs={{0,4},{4,0},{8,12},{12,8},{1,5},{5,1},{9,13},{13,9},{2,6},{6,2},{1... | collective-permute-start | bytes 2949128 | tf_op jit(solution)/shard_map/ppermute | solution.py:205
  128.3 58.2 %collective-permute-start.23 = (bf16[192,2560]{1,0:T(8,128)(2,1)S(1)}, bf16[192,2560]{1,0:T(8,128)(2,1)S(1)}, u32[]{:S(2)}, u32[]{:S(2)}) collective-permute-start(bf16[192,2560]{1,0:T(8,128)(2,1)S(1)} %get-tuple-element.61.rest_0_), channel_id=1, source_target_pairs={{0,8},{4,12},{8,0},{12,4},{1,9},{5,13},{9,1},{13,5},{2,10},{6,14},... | collective-permute-start | bytes 2949128 | tf_op jit(solution)/shard_map/ppermute | solution.py:196
  144.3 42.1 %collective-permute-start.24 = (bf16[192,2560]{1,0:T(8,128)(2,1)S(1)}, bf16[192,2560]{1,0:T(8,128)(2,1)S(1)}, u32[]{:S(2)}, u32[]{:S(2)}) collective-permute-start(bf16[192,2560]{1,0:T(8,128)(2,1)S(1)} %get-tuple-element.61.rest_0_), channel_id=1, source_target_pairs={{0,4},{4,0},{8,12},{12,8},{1,5},{5,1},{9,13},{13,9},{2,6},{6,2},{1... | collective-permute-start | bytes 2949128 | tf_op jit(solution)/shard_map/ppermute | solution.py:205
  165.4 42.2 %collective-permute-start.20 = (bf16[192,2560]{1,0:T(8,128)(2,1)S(1)}, bf16[192,2560]{1,0:T(8,128)(2,1)S(1)}, u32[]{:S(2)}, u32[]{:S(2)}) collective-permute-start(bf16[192,2560]{1,0:T(8,128)(2,1)S(1)} %get-tuple-element.60.rest_0_), channel_id=1, source_target_pairs={{0,8},{4,12},{8,0},{12,4},{1,9},{5,13},{9,1},{13,5},{2,10},{6,14},... | collective-permute-start | bytes 2949128 | tf_op jit(solution)/shard_map/ppermute | solution.py:196
  165.6 42.0 %collective-permute-start.21 = (bf16[192,2560]{1,0:T(8,128)(2,1)S(1)}, bf16[192,2560]{1,0:T(8,128)(2,1)S(1)}, u32[]{:S(2)}, u32[]{:S(2)}) collective-permute-start(bf16[192,2560]{1,0:T(8,128)(2,1)S(1)} %get-tuple-element.60.rest_0_), channel_id=1, source_target_pairs={{0,4},{4,0},{8,12},{12,8},{1,5},{5,1},{9,13},{13,9},{2,6},{6,2},{1... | collective-permute-start | bytes 2949128 | tf_op jit(solution)/shard_map/ppermute | solution.py:205
  178.7 49.9 %collective-permute-start.17 = (bf16[192,2560]{1,0:T(8,128)(2,1)}, bf16[192,2560]{1,0:T(8,128)(2,1)}, u32[]{:S(2)}, u32[]{:S(2)}) collective-permute-start(bf16[192,2560]{1,0:T(8,128)(2,1)} %get-tuple-element.59.rest_0_), channel_id=1, source_target_pairs={{0,8},{4,12},{8,0},{12,4},{1,9},{5,13},{9,1},{13,5},{2,10},{6,14},... | collective-permute-start | bytes 2949128 | tf_op jit(solution)/shard_map/ppermute | solution.py:196
  186.4 42.2 %collective-permute-start.18 = (bf16[192,2560]{1,0:T(8,128)(2,1)}, bf16[192,2560]{1,0:T(8,128)(2,1)}, u32[]{:S(2)}, u32[]{:S(2)}) collective-permute-start(bf16[192,2560]{1,0:T(8,128)(2,1)} %get-tuple-element.59.rest_0_), channel_id=1, source_target_pairs={{0,4},{4,0},{8,12},{12,8},{1,5},{5,1},{9,13},{13,9},{2,6},{6,2},{1... | collective-permute-start | bytes 2949128 | tf_op jit(solution)/shard_map/ppermute | solution.py:205
  186.5 63.3 %collective-permute-start.14 = (bf16[192,2560]{1,0:T(8,128)(2,1)}, bf16[192,2560]{1,0:T(8,128)(2,1)}, u32[]{:S(2)}, u32[]{:S(2)}) collective-permute-start(bf16[192,2560]{1,0:T(8,128)(2,1)} %get-tuple-element.58.rest_0_), channel_id=1, source_target_pairs={{0,8},{4,12},{8,0},{12,4},{1,9},{5,13},{9,1},{13,5},{2,10},{6,14},... | collective-permute-start | bytes 2949128 | tf_op jit(solution)/shard_map/ppermute | solution.py:196
  207.6 42.1 %collective-permute-start.15 = (bf16[192,2560]{1,0:T(8,128)(2,1)}, bf16[192,2560]{1,0:T(8,128)(2,1)}, u32[]{:S(2)}, u32[]{:S(2)}) collective-permute-start(bf16[192,2560]{1,0:T(8,128)(2,1)} %get-tuple-element.58.rest_0_), channel_id=1, source_target_pairs={{0,4},{4,0},{8,12},{12,8},{1,5},{5,1},{9,13},{13,9},{2,6},{6,2},{1... | collective-permute-start | bytes 2949128 | tf_op jit(solution)/shard_map/ppermute | solution.py:205
  207.6 62.6 %collective-permute-start.11 = (bf16[192,2560]{1,0:T(8,128)(2,1)}, bf16[192,2560]{1,0:T(8,128)(2,1)}, u32[]{:S(2)}, u32[]{:S(2)}) collective-permute-start(bf16[192,2560]{1,0:T(8,128)(2,1)} %get-tuple-element.57.rest_0_), channel_id=1, source_target_pairs={{0,8},{4,12},{8,0},{12,4},{1,9},{5,13},{9,1},{13,5},{2,10},{6,14},... | collective-permute-start | bytes 2949128 | tf_op jit(solution)/shard_map/ppermute | solution.py:196
  228.7 41.9 %collective-permute-start.28 = (bf16[192,2560]{1,0:T(8,128)(2,1)}, bf16[192,2560]{1,0:T(8,128)(2,1)S(1)}, u32[]{:S(2)}, u32[]{:S(2)}) collective-permute-start(bf16[192,2560]{1,0:T(8,128)(2,1)} %shard_map.140.rest_1_), channel_id=1, source_target_pairs={{0,4},{4,0},{8,12},{12,8},{1,5},{5,1},{9,13},{13,9},{2,6},{6,2},{1... | collective-permute-start | bytes 2949128 | tf_op jit(solution)/shard_map/ppermute | solution.py:205
  228.7 43.0 %collective-permute-start.31 = (bf16[192,2560]{1,0:T(8,128)(2,1)S(1)}, bf16[192,2560]{1,0:T(8,128)(2,1)S(1)}, u32[]{:S(2)}, u32[]{:S(2)}) collective-permute-start(bf16[192,2560]{1,0:T(8,128)(2,1)S(1)} %copy-done.13), channel_id=1, source_target_pairs={{0,4},{4,0},{8,12},{12,8},{1,5},{5,1},{9,13},{13,9},{2,6},{6,2},{1... | collective-permute-start | bytes 2949128 | tf_op jit(solution)/shard_map/ppermute | solution.py:205
  249.7 23.2 %collective-permute-start.25 = (bf16[192,2560]{1,0:T(8,128)(2,1)}, bf16[192,2560]{1,0:T(8,128)(2,1)S(1)}, u32[]{:S(2)}, u32[]{:S(2)}) collective-permute-start(bf16[192,2560]{1,0:T(8,128)(2,1)} %copy-done.25), channel_id=1, source_target_pairs={{0,4},{4,0},{8,12},{12,8},{1,5},{5,1},{9,13},{13,9},{2,6},{6,2},{1... | collective-permute-start | bytes 2949128 | tf_op jit(solution)/shard_map/ppermute | solution.py:205
  249.8 25.3 %collective-permute-start.22 = (bf16[192,2560]{1,0:T(8,128)(2,1)}, bf16[192,2560]{1,0:T(8,128)(2,1)S(1)}, u32[]{:S(2)}, u32[]{:S(2)}) collective-permute-start(bf16[192,2560]{1,0:T(8,128)(2,1)} %copy-done.33), channel_id=1, source_target_pairs={{0,4},{4,0},{8,12},{12,8},{1,5},{5,1},{9,13},{13,9},{2,6},{6,2},{1... | collective-permute-start | bytes 2949128 | tf_op jit(solution)/shard_map/ppermute | solution.py:205
  271.5 32.0 %collective-permute-start.16 = (bf16[192,2560]{1,0:T(8,128)(2,1)}, bf16[192,2560]{1,0:T(8,128)(2,1)}, u32[]{:S(2)}, u32[]{:S(2)}) collective-permute-start(bf16[192,2560]{1,0:T(8,128)(2,1)} %collective-permute-done.14.rest_1_), channel_id=1, source_target_pairs={{0,4},{4,0},{8,12},{12,8},{1,5},{5,1},{9,13},{13,9},{2,6},{6,2},{1... | collective-permute-start | bytes 2949128 | tf_op jit(solution)/shard_map/ppermute | solution.py:205
  272.6 35.6 %collective-permute-start.12 = (bf16[192,2560]{1,0:T(8,128)(2,1)}, bf16[192,2560]{1,0:T(8,128)(2,1)}, u32[]{:S(2)}, u32[]{:S(2)}) collective-permute-start(bf16[192,2560]{1,0:T(8,128)(2,1)} %get-tuple-element.57.rest_0_), channel_id=1, source_target_pairs={{0,4},{4,0},{8,12},{12,8},{1,5},{5,1},{9,13},{13,9},{2,6},{6,2},{1... | collective-permute-start | bytes 2949128 | tf_op jit(solution)/shard_map/ppermute | solution.py:205
  273.9 34.5 %collective-permute-start.34 = (bf16[192,2560]{1,0:T(8,128)(2,1)}, bf16[192,2560]{1,0:T(8,128)(2,1)}, u32[]{:S(2)}, u32[]{:S(2)}) collective-permute-start(bf16[192,2560]{1,0:T(8,128)(2,1)} %copy-done.27), channel_id=1, source_target_pairs={{0,8},{4,12},{8,0},{12,4},{1,9},{5,13},{9,1},{13,5},{2,10},{6,14},... | collective-permute-start | bytes 2949128 | tf_op jit(solution)/shard_map/ppermute | solution.py:196
  276.0 32.8 %collective-permute-start.13 = (bf16[192,2560]{1,0:T(8,128)(2,1)}, bf16[192,2560]{1,0:T(8,128)(2,1)}, u32[]{:S(2)}, u32[]{:S(2)}) collective-permute-start(bf16[192,2560]{1,0:T(8,128)(2,1)} %collective-permute-done.11.rest_1_), channel_id=1, source_target_pairs={{0,4},{4,0},{8,12},{12,8},{1,5},{5,1},{9,13},{13,9},{2,6},{6,2},{1... | collective-permute-start | bytes 2949128 | tf_op jit(solution)/shard_map/ppermute | solution.py:205
  277.3 41.1 %collective-permute-start.10 = (bf16[192,2560]{1,0:T(8,128)(2,1)}, bf16[192,2560]{1,0:T(8,128)(2,1)S(1)}, u32[]{:S(2)}, u32[]{:S(2)}) collective-permute-start(bf16[192,2560]{1,0:T(8,128)(2,1)} %copy-done.4), channel_id=1, source_target_pairs={{0,8},{4,12},{8,0},{12,4},{1,9},{5,13},{9,1},{13,5},{2,10},{6,14},... | collective-permute-start | bytes 2949128 | tf_op jit(solution)/shard_map/ppermute | solution.py:196
  303.5 16.9 %collective-permute-start.35 = (bf16[192,2560]{1,0:T(8,128)(2,1)S(1)}, bf16[192,2560]{1,0:T(8,128)(2,1)}, u32[]{:S(2)}, u32[]{:S(2)}) collective-permute-start(bf16[192,2560]{1,0:T(8,128)(2,1)S(1)} %copy-done.28), channel_id=1, source_target_pairs={{0,4},{4,0},{8,12},{12,8},{1,5},{5,1},{9,13},{13,9},{2,6},{6,2},{1... | collective-permute-start | bytes 2949128 | tf_op jit(solution)/shard_map/ppermute | solution.py:205
  308.3 16.8 %collective-permute-start.32 = (bf16[192,2560]{1,0:T(8,128)(2,1)S(1)}, bf16[192,2560]{1,0:T(8,128)(2,1)}, u32[]{:S(2)}, u32[]{:S(2)}) collective-permute-start(bf16[192,2560]{1,0:T(8,128)(2,1)S(1)} %copy-done.5), channel_id=1, source_target_pairs={{0,4},{4,0},{8,12},{12,8},{1,5},{5,1},{9,13},{13,9},{2,6},{6,2},{1... | collective-permute-start | bytes 2949128 | tf_op jit(solution)/shard_map/ppermute | solution.py:205
  308.5 11.9 %collective-permute-start.36 = (bf16[192,2560]{1,0:T(8,128)(2,1)}, bf16[192,2560]{1,0:T(8,128)(2,1)}, u32[]{:S(2)}, u32[]{:S(2)}) collective-permute-start(bf16[192,2560]{1,0:T(8,128)(2,1)} %collective-permute-done.34.rest_1_), channel_id=1, source_target_pairs={{0,4},{4,0},{8,12},{12,8},{1,5},{5,1},{9,13},{13,9},{2,6},{6,2},{1... | collective-permute-start | bytes 2949128 | tf_op jit(solution)/shard_map/ppermute | solution.py:205
  (54 other events, 493.1 us)
